TPU v7x, 768 devices: a whole 4x8x12 slice. The times are simulated.
768 devices in a mesh: blk: 32 (over y_hi, x, core), grp: 24 (over z, y_lo).
Axes of the slice: x: 4, y: 8 (y_hi: 4, y_lo: 2; y = y_hi * 2 + y_lo), z: 12, core: 2. Of those that a mesh axis runs over, the one named last changes fastest.
Arguments:
- picture_embedding_array: bfloat16 [196608, 1152], P(('blk', 'grp')), may hold values from -0.1875 to 0.1875
- caption_embedding_array: bfloat16 [196608, 1152], P(('blk', 'grp')), may hold values from -0.1875 to 0.1875
- sharpness_multiplier: float32 [1], replicated, may hold values from 8 to 16
- score_offset: float32 [1], replicated, may hold values from -6 to -3
Outputs:
- row_loss: float32 [196608], P(('blk', 'grp'))
- grad_images: float32 [196608, 1152], P(('blk', 'grp'))
- grad_texts: float32 [196608, 1152], P(('blk', 'grp'))
All inputs are finite; a program needn't handle non-finite values.
Results may differ from a plain program's by a relative error of at most 0.02.
Values may be sent and summed in bfloat16 or wider, within the bound.
No kernel may reach another device: no remote copies, remote signals or barrier semaphores. Data moves between devices by JAX's collectives and lax.ppermute only.
A program may use at most 32 MiB of HBM per device.

v0:
```python
import jax
import jax.numpy as jnp
from jax import lax
from jax.sharding import PartitionSpec as P

KSTEPS = 8


def passed_along(block, axis, distance):
    devices = range(lax.axis_size(axis))
    route = [((i - distance) % len(devices), i) for i in devices]
    return lax.ppermute(block, axis, route)


def normalize(raw):
    computed_quantities = raw.astype(jnp.float32)
    inverse = lax.rsqrt(
        jnp.sum(computed_quantities * computed_quantities, axis=-1, keepdims=True) + 1e-06
    )
    return (computed_quantities * inverse, inverse)


def back_norm(unit32, inverse, grad_unit):
    along = jnp.sum(unit32 * grad_unit, axis=-1, keepdims=True)
    return inverse * (grad_unit - unit32 * along)


def pairwise_loss_terms(
    image_block_rows, text_block_rows, target_labels, smoothing_coefficient, block_displacement
):
    pair_logit_matrix = (
        smoothing_coefficient
        * lax.dot_general(
            image_block_rows,
            text_block_rows,
            (((1,), (1,)), ((), ())),
            preferred_element_type=jnp.float32,
        )
        + block_displacement
    )
    row_portion = jnp.sum(jax.nn.softplus(-target_labels * pair_logit_matrix), axis=-1)
    sigmoid_weights = (
        -target_labels * jax.nn.sigmoid(-target_labels * pair_logit_matrix) * smoothing_coefficient
    ).astype(jnp.bfloat16)
    return (row_portion, sigmoid_weights)


def image_side(sigmoid_weights, text_block_rows):
    return jnp.dot(sigmoid_weights, text_block_rows, preferred_element_type=jnp.float32)


def text_side(sigmoid_weights, image_block_rows):
    return lax.dot_general(
        sigmoid_weights,
        image_block_rows,
        (((0,), (0,)), ((), ())),
        preferred_element_type=jnp.float32,
    )


def on_device(picture_embedding_array, caption_embedding_array, sharpness_multiplier, score_offset):
    smoothing_coefficient = sharpness_multiplier[0]
    block_displacement = score_offset[0]
    rows = picture_embedding_array.shape[0]
    img_unit32, img_inverse = normalize(picture_embedding_array)
    txt_unit32, txt_inverse = normalize(caption_embedding_array)
    image_unit_vectors = img_unit32.astype(jnp.bfloat16)
    text_unit_vectors = txt_unit32.astype(jnp.bfloat16)
    positions = lax.broadcasted_iota(jnp.int32, (rows, rows), 0)
    columns = lax.broadcasted_iota(jnp.int32, (rows, rows), 1)
    initial_label_values = jnp.where(positions == columns, 1.0, -1.0).astype(jnp.float32)
    negative_labels = jnp.full((rows, rows), -1.0, jnp.float32)
    row_total_sum, sigmoid_weights = pairwise_loss_terms(
        image_unit_vectors,
        text_unit_vectors,
        initial_label_values,
        smoothing_coefficient,
        block_displacement,
    )
    grad_img = image_side(sigmoid_weights, text_unit_vectors)
    own_text = text_side(sigmoid_weights, image_unit_vectors)
    incoming_caption_groups = text_unit_vectors
    carried = own_text
    for hop_index in range(1, KSTEPS):
        incoming_caption_groups, carried = (
            passed_along(incoming_caption_groups, ("blk", "grp"), 1),
            passed_along(carried.astype(jnp.bfloat16), ("blk", "grp"), 1).astype(carried.dtype),
        )
        row_portion, sigmoid_weights = pairwise_loss_terms(
            image_unit_vectors,
            incoming_caption_groups,
            negative_labels,
            smoothing_coefficient,
            block_displacement,
        )
        row_total_sum = row_total_sum + row_portion
        grad_img = grad_img + image_side(sigmoid_weights, incoming_caption_groups)
        carried = carried + text_side(sigmoid_weights, image_unit_vectors)
    grad_txt = passed_along(carried.astype(jnp.bfloat16), ("blk", "grp"), 1 - KSTEPS).astype(
        carried.dtype
    )
    grad_images = back_norm(img_unit32, img_inverse, grad_img)
    grad_texts = back_norm(txt_unit32, txt_inverse, grad_txt)
    return (row_total_sum, grad_images, grad_texts)


def solution(mesh):
    return jax.shard_map(
        on_device,
        mesh=mesh,
        in_specs=(P(("blk", "grp"), None), P(("blk", "grp"), None), P(), P()),
        out_specs=(P(("blk", "grp")), P(("blk", "grp"), None), P(("blk", "grp"), None)),
        check_vma=False,
    )
```

profile of v0, /device:TPU:1, one launch (start us, length us, event | category | flops | bytes accessed | tf_op | source)
XLA Modules:
  0.0 248.8 jit_solution(5001974043479104331)
XLA Ops:
  0.6 1.3 fusion.9
  2.0 1.2 fusion.1
  3.2 4.0 %collective-permute-start = (bf16[256,1152]{1,0:T(8,128)(2,1)S(1)}, bf16[256,1152]{1,0:T(8,128)(2,1)S(1)}, u32[]{:S(2)}, u32[]{:S(2)}) collective-permute-start(bf16[256,1152]{1,0:T(8,128)(2,1)S(1)} %fusion.1), channel_id=1, source_target_pairs={{767,0},{0,1},{1,2},{2,3},{3,4},{4,5},{5,6},{6,7},{7,8},{8,9},{9,1... | collective-permute-start | bytes 1769480 | tf_op jit(solution)/shard_map/ppermute | solution.py:12
  7.9 0.2 fusion.8
  8.8 0.6 fusion.21
  9.4 0.5 convolution_convert_fusion
  9.8 3.9 %collective-permute-start.7 = (bf16[256,1152]{1,0:T(8,128)(2,1)S(1)}, bf16[256,1152]{1,0:T(8,128)(2,1)S(1)}, u32[]{:S(2)}, u32[]{:S(2)}) collective-permute-start(bf16[256,1152]{1,0:T(8,128)(2,1)S(1)} %convolution_convert_fusion), channel_id=1, source_target_pairs={{767,0},{0,1},{1,2},{2,3},{3,4},{4,5},{5,6},{6,7},{7,8},{8,9},{9,1... | collective-permute-start | bytes 1769480 | tf_op jit(solution)/shard_map/ppermute | solution.py:12
  13.7 0.4 fusion.36
  14.1 19.9 %collective-permute-done = bf16[256,1152]{1,0:T(8,128)(2,1)S(1)} collective-permute-done((bf16[256,1152]{1,0:T(8,128)(2,1)S(1)}, bf16[256,1152]{1,0:T(8,128)(2,1)S(1)}, u32[]{:S(2)}, u32[]{:S(2)}) %collective-permute-start) | collective-permute-done | bytes 589856 | tf_op jit(solution)/shard_map/ppermute | solution.py:12
  34.1 1.9 collective-permute-start.1
  36.0 0.6 fusion.22
  36.6 10.1 %collective-permute-done.7 = bf16[256,1152]{1,0:T(8,128)(2,1)S(1)} collective-permute-done((bf16[256,1152]{1,0:T(8,128)(2,1)S(1)}, bf16[256,1152]{1,0:T(8,128)(2,1)S(1)}, u32[]{:S(2)}, u32[]{:S(2)}) %collective-permute-start.7) | collective-permute-done | bytes 589856 | tf_op jit(solution)/shard_map/ppermute | solution.py:12
  46.7 0.4 add_convert_fusion.6
  47.1 1.9 collective-permute-start.8
  49.1 0.4 convolution_add_fusion.6
  49.5 9.9 %collective-permute-done.1 = bf16[256,1152]{1,0:T(8,128)(2,1)S(1)} collective-permute-done((bf16[256,1152]{1,0:T(8,128)(2,1)S(1)}, bf16[256,1152]{1,0:T(8,128)(2,1)S(1)}, u32[]{:S(2)}, u32[]{:S(2)}) %collective-permute-start.1) | collective-permute-done | bytes 589856 | tf_op jit(solution)/shard_map/ppermute | solution.py:12
  59.3 1.9 collective-permute-start.2
  61.3 0.6 fusion.23
  61.8 0.4 fusion.30
  62.3 9.7 %collective-permute-done.8 = bf16[256,1152]{1,0:T(8,128)(2,1)S(1)} collective-permute-done((bf16[256,1152]{1,0:T(8,128)(2,1)S(1)}, bf16[256,1152]{1,0:T(8,128)(2,1)S(1)}, u32[]{:S(2)}, u32[]{:S(2)}) %collective-permute-start.8) | collective-permute-done | bytes 589856 | tf_op jit(solution)/shard_map/ppermute | solution.py:12
  72.1 1.9 collective-permute-start.9
  74.0 0.4 convolution_add_fusion.5
  74.4 10.2 %collective-permute-done.2 = bf16[256,1152]{1,0:T(8,128)(2,1)S(1)} collective-permute-done((bf16[256,1152]{1,0:T(8,128)(2,1)S(1)}, bf16[256,1152]{1,0:T(8,128)(2,1)S(1)}, u32[]{:S(2)}, u32[]{:S(2)}) %collective-permute-start.2) | collective-permute-done | bytes 589856 | tf_op jit(solution)/shard_map/ppermute | solution.py:12
  84.6 1.9 collective-permute-start.3
  86.5 0.6 fusion.24
  87.1 0.4 fusion.31
  87.6 9.7 %collective-permute-done.9 = bf16[256,1152]{1,0:T(8,128)(2,1)S(1)} collective-permute-done((bf16[256,1152]{1,0:T(8,128)(2,1)S(1)}, bf16[256,1152]{1,0:T(8,128)(2,1)S(1)}, u32[]{:S(2)}, u32[]{:S(2)}) %collective-permute-start.9) | collective-permute-done | bytes 589856 | tf_op jit(solution)/shard_map/ppermute | solution.py:12
  97.3 0.1 add_convert_fusion.4
  97.4 1.9 collective-permute-start.10
  99.3 0.4 convolution_add_fusion.4
  99.7 10.2 %collective-permute-done.3 = bf16[256,1152]{1,0:T(8,128)(2,1)S(1)} collective-permute-done((bf16[256,1152]{1,0:T(8,128)(2,1)S(1)}, bf16[256,1152]{1,0:T(8,128)(2,1)S(1)}, u32[]{:S(2)}, u32[]{:S(2)}) %collective-permute-start.3) | collective-permute-done | bytes 589856 | tf_op jit(solution)/shard_map/ppermute | solution.py:12
  109.9 1.9 collective-permute-start.4
  111.8 0.6 fusion.25
  112.4 0.4 fusion.32
  112.9 9.7 %collective-permute-done.10 = bf16[256,1152]{1,0:T(8,128)(2,1)S(1)} collective-permute-done((bf16[256,1152]{1,0:T(8,128)(2,1)S(1)}, bf16[256,1152]{1,0:T(8,128)(2,1)S(1)}, u32[]{:S(2)}, u32[]{:S(2)}) %collective-permute-start.10) | collective-permute-done | bytes 589856 | tf_op jit(solution)/shard_map/ppermute | solution.py:12
  122.5 0.1 add_convert_fusion.3
  122.6 1.9 collective-permute-start.11
  124.6 0.4 convolution_add_fusion.3
  125.0 10.2 %collective-permute-done.4 = bf16[256,1152]{1,0:T(8,128)(2,1)S(1)} collective-permute-done((bf16[256,1152]{1,0:T(8,128)(2,1)S(1)}, bf16[256,1152]{1,0:T(8,128)(2,1)S(1)}, u32[]{:S(2)}, u32[]{:S(2)}) %collective-permute-start.4) | collective-permute-done | bytes 589856 | tf_op jit(solution)/shard_map/ppermute | solution.py:12
  135.2 1.9 collective-permute-start.5
  137.1 0.6 fusion.26
  137.7 0.4 fusion.33
  138.1 9.7 %collective-permute-done.11 = bf16[256,1152]{1,0:T(8,128)(2,1)S(1)} collective-permute-done((bf16[256,1152]{1,0:T(8,128)(2,1)S(1)}, bf16[256,1152]{1,0:T(8,128)(2,1)S(1)}, u32[]{:S(2)}, u32[]{:S(2)}) %collective-permute-start.11) | collective-permute-done | bytes 589856 | tf_op jit(solution)/shard_map/ppermute | solution.py:12
  147.8 0.1 add_convert_fusion.2
  147.9 1.9 collective-permute-start.12
  149.9 0.4 convolution_add_fusion.2
  150.3 10.2 %collective-permute-done.5 = bf16[256,1152]{1,0:T(8,128)(2,1)S(1)} collective-permute-done((bf16[256,1152]{1,0:T(8,128)(2,1)S(1)}, bf16[256,1152]{1,0:T(8,128)(2,1)S(1)}, u32[]{:S(2)}, u32[]{:S(2)}) %collective-permute-start.5) | collective-permute-done | bytes 589856 | tf_op jit(solution)/shard_map/ppermute | solution.py:12
  160.5 1.9 collective-permute-start.6
  162.4 0.6 fusion.27
  163.0 0.4 fusion.34
  163.4 9.7 %collective-permute-done.12 = bf16[256,1152]{1,0:T(8,128)(2,1)S(1)} collective-permute-done((bf16[256,1152]{1,0:T(8,128)(2,1)S(1)}, bf16[256,1152]{1,0:T(8,128)(2,1)S(1)}, u32[]{:S(2)}, u32[]{:S(2)}) %collective-permute-start.12) | collective-permute-done | bytes 589856 | tf_op jit(solution)/shard_map/ppermute | solution.py:12
  173.2 2.1 collective-permute-start.13
  175.3 0.4 convolution_add_fusion.1
  175.7 10.0 %collective-permute-done.6 = bf16[256,1152]{1,0:T(8,128)(2,1)S(1)} collective-permute-done((bf16[256,1152]{1,0:T(8,128)(2,1)S(1)}, bf16[256,1152]{1,0:T(8,128)(2,1)S(1)}, u32[]{:S(2)}, u32[]{:S(2)}) %collective-permute-start.6) | collective-permute-done | bytes 589856 | tf_op jit(solution)/shard_map/ppermute | solution.py:12
  185.7 0.6 fusion.28
  186.3 0.4 fusion.35
  186.8 10.8 %collective-permute-done.13 = bf16[256,1152]{1,0:T(8,128)(2,1)S(1)} collective-permute-done((bf16[256,1152]{1,0:T(8,128)(2,1)S(1)}, bf16[256,1152]{1,0:T(8,128)(2,1)S(1)}, u32[]{:S(2)}, u32[]{:S(2)}) %collective-permute-start.13) | collective-permute-done | bytes 589856 | tf_op jit(solution)/shard_map/ppermute | solution.py:12
  197.7 3.6 %collective-permute-start.14 = (bf16[256,1152]{1,0:T(8,128)(2,1)S(1)}, bf16[256,1152]{1,0:T(8,128)(2,1)S(1)}, u32[]{:S(2)}, u32[]{:S(2)}) collective-permute-start(bf16[256,1152]{1,0:T(8,128)(2,1)S(1)} %add_convert_fusion), channel_id=1, source_target_pairs={{7,0},{8,1},{9,2},{10,3},{11,4},{12,5},{13,6},{14,7},{15,8},{16,9}... | collective-permute-start | bytes 1769480 | tf_op jit(solution)/shard_map/ppermute | solution.py:12
  201.3 0.5 fusion.5
  201.8 0.6 add_add_fusion
  202.4 1.3 fusion.7
  203.6 43.5 %collective-permute-done.14 = bf16[256,1152]{1,0:T(8,128)(2,1)S(1)} collective-permute-done((bf16[256,1152]{1,0:T(8,128)(2,1)S(1)}, bf16[256,1152]{1,0:T(8,128)(2,1)S(1)}, u32[]{:S(2)}, u32[]{:S(2)}) %collective-permute-start.14) | collective-permute-done | bytes 589856 | tf_op jit(solution)/shard_map/ppermute | solution.py:12
  247.1 0.3 fusion.10
  247.5 1.3 fusion.11
  (9 shorter events, 0.3 us)
Async XLA Ops:
  0.6 7.3 %copy-start = (bf16[256,1152]{1,0:T(8,128)(2,1)S(1)}, bf16[256,1152]{1,0:T(8,128)(2,1)}, u32[]{:S(2)}) copy-start(bf16[256,1152]{1,0:T(8,128)(2,1)} %param.4) | copy-start | bytes 1769476
  3.2 30.9 %collective-permute-start = (bf16[256,1152]{1,0:T(8,128)(2,1)S(1)}, bf16[256,1152]{1,0:T(8,128)(2,1)S(1)}, u32[]{:S(2)}, u32[]{:S(2)}) collective-permute-start(bf16[256,1152]{1,0:T(8,128)(2,1)S(1)} %fusion.1), channel_id=1, source_target_pairs={{767,0},{0,1},{1,2},{2,3},{3,4},{4,5},{5,6},{6,7},{7,8},{8,9},{9,1... | collective-permute-start | bytes 1769480 | tf_op jit(solution)/shard_map/ppermute | solution.py:12
  9.8 36.9 %collective-permute-start.7 = (bf16[256,1152]{1,0:T(8,128)(2,1)S(1)}, bf16[256,1152]{1,0:T(8,128)(2,1)S(1)}, u32[]{:S(2)}, u32[]{:S(2)}) collective-permute-start(bf16[256,1152]{1,0:T(8,128)(2,1)S(1)} %convolution_convert_fusion), channel_id=1, source_target_pairs={{767,0},{0,1},{1,2},{2,3},{3,4},{4,5},{5,6},{6,7},{7,8},{8,9},{9,1... | collective-permute-start | bytes 1769480 | tf_op jit(solution)/shard_map/ppermute | solution.py:12
  34.1 25.3 %collective-permute-start.1 = (bf16[256,1152]{1,0:T(8,128)(2,1)S(1)}, bf16[256,1152]{1,0:T(8,128)(2,1)S(1)}, u32[]{:S(2)}, u32[]{:S(2)}) collective-permute-start(bf16[256,1152]{1,0:T(8,128)(2,1)S(1)} %collective-permute-done), channel_id=1, source_target_pairs={{767,0},{0,1},{1,2},{2,3},{3,4},{4,5},{5,6},{6,7},{7,8},{8,9},{9,1... | collective-permute-start | bytes 1769480 | tf_op jit(solution)/shard_map/ppermute | solution.py:12
  47.1 24.8 %collective-permute-start.8 = (bf16[256,1152]{1,0:T(8,128)(2,1)S(1)}, bf16[256,1152]{1,0:T(8,128)(2,1)S(1)}, u32[]{:S(2)}, u32[]{:S(2)}) collective-permute-start(bf16[256,1152]{1,0:T(8,128)(2,1)S(1)} %add_convert_fusion.6), channel_id=1, source_target_pairs={{767,0},{0,1},{1,2},{2,3},{3,4},{4,5},{5,6},{6,7},{7,8},{8,9},{9,1... | collective-permute-start | bytes 1769480 | tf_op jit(solution)/shard_map/ppermute | solution.py:12
  59.3 25.3 %collective-permute-start.2 = (bf16[256,1152]{1,0:T(8,128)(2,1)S(1)}, bf16[256,1152]{1,0:T(8,128)(2,1)S(1)}, u32[]{:S(2)}, u32[]{:S(2)}) collective-permute-start(bf16[256,1152]{1,0:T(8,128)(2,1)S(1)} %collective-permute-done.1), channel_id=1, source_target_pairs={{767,0},{0,1},{1,2},{2,3},{3,4},{4,5},{5,6},{6,7},{7,8},{8,9},{9,1... | collective-permute-start | bytes 1769480 | tf_op jit(solution)/shard_map/ppermute | solution.py:12
  72.1 25.2 %collective-permute-start.9 = (bf16[256,1152]{1,0:T(8,128)(2,1)S(1)}, bf16[256,1152]{1,0:T(8,128)(2,1)S(1)}, u32[]{:S(2)}, u32[]{:S(2)}) collective-permute-start(bf16[256,1152]{1,0:T(8,128)(2,1)S(1)} %add_convert_fusion.5), channel_id=1, source_target_pairs={{767,0},{0,1},{1,2},{2,3},{3,4},{4,5},{5,6},{6,7},{7,8},{8,9},{9,1... | collective-permute-start | bytes 1769480 | tf_op jit(solution)/shard_map/ppermute | solution.py:12
  84.6 25.3 %collective-permute-start.3 = (bf16[256,1152]{1,0:T(8,128)(2,1)S(1)}, bf16[256,1152]{1,0:T(8,128)(2,1)S(1)}, u32[]{:S(2)}, u32[]{:S(2)}) collective-permute-start(bf16[256,1152]{1,0:T(8,128)(2,1)S(1)} %collective-permute-done.2), channel_id=1, source_target_pairs={{767,0},{0,1},{1,2},{2,3},{3,4},{4,5},{5,6},{6,7},{7,8},{8,9},{9,1... | collective-permute-start | bytes 1769480 | tf_op jit(solution)/shard_map/ppermute | solution.py:12
  97.4 25.2 %collective-permute-start.10 = (bf16[256,1152]{1,0:T(8,128)(2,1)S(1)}, bf16[256,1152]{1,0:T(8,128)(2,1)S(1)}, u32[]{:S(2)}, u32[]{:S(2)}) collective-permute-start(bf16[256,1152]{1,0:T(8,128)(2,1)S(1)} %add_convert_fusion.4), channel_id=1, source_target_pairs={{767,0},{0,1},{1,2},{2,3},{3,4},{4,5},{5,6},{6,7},{7,8},{8,9},{9,1... | collective-permute-start | bytes 1769480 | tf_op jit(solution)/shard_map/ppermute | solution.py:12
  109.9 25.3 %collective-permute-start.4 = (bf16[256,1152]{1,0:T(8,128)(2,1)S(1)}, bf16[256,1152]{1,0:T(8,128)(2,1)S(1)}, u32[]{:S(2)}, u32[]{:S(2)}) collective-permute-start(bf16[256,1152]{1,0:T(8,128)(2,1)S(1)} %collective-permute-done.3), channel_id=1, source_target_pairs={{767,0},{0,1},{1,2},{2,3},{3,4},{4,5},{5,6},{6,7},{7,8},{8,9},{9,1... | collective-permute-start | bytes 1769480 | tf_op jit(solution)/shard_map/ppermute | solution.py:12
  122.6 25.2 %collective-permute-start.11 = (bf16[256,1152]{1,0:T(8,128)(2,1)S(1)}, bf16[256,1152]{1,0:T(8,128)(2,1)S(1)}, u32[]{:S(2)}, u32[]{:S(2)}) collective-permute-start(bf16[256,1152]{1,0:T(8,128)(2,1)S(1)} %add_convert_fusion.3), channel_id=1, source_target_pairs={{767,0},{0,1},{1,2},{2,3},{3,4},{4,5},{5,6},{6,7},{7,8},{8,9},{9,1... | collective-permute-start | bytes 1769480 | tf_op jit(solution)/shard_map/ppermute | solution.py:12
  135.2 25.3 %collective-permute-start.5 = (bf16[256,1152]{1,0:T(8,128)(2,1)S(1)}, bf16[256,1152]{1,0:T(8,128)(2,1)S(1)}, u32[]{:S(2)}, u32[]{:S(2)}) collective-permute-start(bf16[256,1152]{1,0:T(8,128)(2,1)S(1)} %collective-permute-done.4), channel_id=1, source_target_pairs={{767,0},{0,1},{1,2},{2,3},{3,4},{4,5},{5,6},{6,7},{7,8},{8,9},{9,1... | collective-permute-start | bytes 1769480 | tf_op jit(solution)/shard_map/ppermute | solution.py:12
  147.9 25.2 %collective-permute-start.12 = (bf16[256,1152]{1,0:T(8,128)(2,1)S(1)}, bf16[256,1152]{1,0:T(8,128)(2,1)S(1)}, u32[]{:S(2)}, u32[]{:S(2)}) collective-permute-start(bf16[256,1152]{1,0:T(8,128)(2,1)S(1)} %add_convert_fusion.2), channel_id=1, source_target_pairs={{767,0},{0,1},{1,2},{2,3},{3,4},{4,5},{5,6},{6,7},{7,8},{8,9},{9,1... | collective-permute-start | bytes 1769480 | tf_op jit(solution)/shard_map/ppermute | solution.py:12
  160.5 25.3 %collective-permute-start.6 = (bf16[256,1152]{1,0:T(8,128)(2,1)S(1)}, bf16[256,1152]{1,0:T(8,128)(2,1)S(1)}, u32[]{:S(2)}, u32[]{:S(2)}) collective-permute-start(bf16[256,1152]{1,0:T(8,128)(2,1)S(1)} %collective-permute-done.5), channel_id=1, source_target_pairs={{767,0},{0,1},{1,2},{2,3},{3,4},{4,5},{5,6},{6,7},{7,8},{8,9},{9,1... | collective-permute-start | bytes 1769480 | tf_op jit(solution)/shard_map/ppermute | solution.py:12
  173.2 24.3 %collective-permute-start.13 = (bf16[256,1152]{1,0:T(8,128)(2,1)S(1)}, bf16[256,1152]{1,0:T(8,128)(2,1)S(1)}, u32[]{:S(2)}, u32[]{:S(2)}) collective-permute-start(bf16[256,1152]{1,0:T(8,128)(2,1)S(1)} %add_convert_fusion.1), channel_id=1, source_target_pairs={{767,0},{0,1},{1,2},{2,3},{3,4},{4,5},{5,6},{6,7},{7,8},{8,9},{9,1... | collective-permute-start | bytes 1769480 | tf_op jit(solution)/shard_map/ppermute | solution.py:12
  197.7 49.5 %collective-permute-start.14 = (bf16[256,1152]{1,0:T(8,128)(2,1)S(1)}, bf16[256,1152]{1,0:T(8,128)(2,1)S(1)}, u32[]{:S(2)}, u32[]{:S(2)}) collective-permute-start(bf16[256,1152]{1,0:T(8,128)(2,1)S(1)} %add_convert_fusion), channel_id=1, source_target_pairs={{7,0},{8,1},{9,2},{10,3},{11,4},{12,5},{13,6},{14,7},{15,8},{16,9}... | collective-permute-start | bytes 1769480 | tf_op jit(solution)/shard_map/ppermute | solution.py:12
  202.4 44.8 %copy-start.1 = (bf16[256,1152]{1,0:T(8,128)(2,1)S(1)}, bf16[256,1152]{1,0:T(8,128)(2,1)}, u32[]{:S(2)}) copy-start(bf16[256,1152]{1,0:T(8,128)(2,1)} %param.5) | copy-start | bytes 1769476
where the time goes:
time: 253 us; the launch traced here: 249 us
  waiting for transfers between devices  193 us (76%)
  starting transfers between devices  34.7 us (14%)
  matrix products  11.6 us (5%)
  other arithmetic  6.88 us (3%)
    ppermute x15, waiting for transfers between devices, passed_along(): return lax.ppermute(block, axis, route)  193 us
    ppermute x15, starting transfers between devices, passed_along(): return lax.ppermute(block, axis, route)  34.7 us
  transfers between devices with their start and end apart: 15, of which 15 were waited for; matrix products, arithmetic and copies ran while one was open for 6% of the time, Pallas kernels for 0%

commit v1 on v0

v1 whole, which is shorter than its diff:
```python
import functools

import jax
import jax.numpy as jnp
from jax import lax
from jax.experimental import pallas as pl
from jax.experimental.pallas import tpu as pltpu
from jax.sharding import PartitionSpec as P

AXES = ("blk", "grp")
BF16 = jnp.bfloat16
F32 = jnp.float32
EXTRA = 128


def vmem(count):
    return [pl.BlockSpec(memory_space=pltpu.VMEM)] * count


def smem(count):
    return [pl.BlockSpec(memory_space=pltpu.SMEM)] * count


def unit_and_inverse(raw):
    wide = raw.astype(F32)
    inverse = lax.rsqrt(jnp.sum(wide * wide, axis=-1, keepdims=True) + 1e-06)
    return wide * inverse, inverse


def prepare_kernel(flags, images, texts, x, y, both):
    rows = images.shape[0]
    img = unit_and_inverse(images[...])[0].astype(BF16)
    txt = unit_and_inverse(texts[...])[0].astype(BF16)
    even = flags[1] == 0

    @pl.when(even)
    def _():
        x[...] = txt
        both[:rows] = txt
        y[...] = img
        both[rows:] = img

    @pl.when(jnp.logical_not(even))
    def _():
        x[...] = img
        both[:rows] = img
        y[...] = txt
        both[rows:] = txt


def pair(scalars, rows, columns, diagonal):
    scale, offset = scalars[0], scalars[1]
    logits = (
        scale
        * lax.dot_general(rows, columns, (((1,), (1,)), ((), ())), preferred_element_type=F32)
        + offset
    )
    if diagonal:
        i = lax.broadcasted_iota(jnp.int32, logits.shape, 0)
        j = lax.broadcasted_iota(jnp.int32, logits.shape, 1)
        negated = jnp.where(i == j, -1.0, 1.0).astype(F32)
        logits = negated * logits
    small = jnp.exp(-jnp.abs(logits))
    share = 1.0 / (1.0 + small)
    sigmoid = jnp.where(logits >= 0, share, small * share)
    weights = sigmoid * scale
    if diagonal:
        weights = negated * weights
    loss = jnp.sum(jnp.maximum(logits, 0.0) + jnp.log1p(small), axis=-1, keepdims=True)
    return jnp.dot(weights.astype(BF16), columns, preferred_element_type=F32), loss


def early_kernel(
    flags, scalars, mine, other, x1, y1, x2, y2, acc_x, acc_y, loss_mine, loss_other
):
    rows = x1.shape[0]
    x_mine, y_mine = mine.at[:rows], mine.at[rows:]
    y_other, x_other = other.at[:rows], other.at[rows:]

    def side(own, own_columns, theirs, their_columns):
        total, loss = None, None
        for columns, diagonal in own_columns:
            grad, term = pair(scalars, own[...], columns[...], diagonal)
            total = grad if total is None else total + grad
            loss = term if loss is None else loss + term
        total_other, loss_other_ = None, None
        for columns in their_columns:
            grad, term = pair(scalars, theirs[...], columns[...], False)
            total_other = grad if total_other is None else total_other + grad
            loss_other_ = term if loss_other_ is None else loss_other_ + term
        return total, loss, total_other, loss_other_

    a, la, b, lb = side(x_mine, [(y_mine, True), (y1, False), (y2, False)], x_other, [y1, y2])
    acc_x[0] = a
    acc_x[1] = b
    a, lc, b, ld = side(
        y_mine, [(x_mine, True), (x1, False), (x2, False)], y_other, [x_mine, x1, x2]
    )
    acc_y[0] = a
    acc_y[1] = b
    images_are_y = flags[0] == 0
    loss_mine[...] = jnp.where(images_are_y, lc, la)
    loss_other[...] = jnp.where(images_are_y, ld, lb)


def y3_kernel(
    flags, scalars, mine, other, y3, acc_x, loss_mine, loss_other, new_x, new_mine, new_other
):
    rows = y3.shape[0]
    images_are_y = flags[0] == 0
    grad, loss = pair(scalars, mine[:rows], y3[...], False)
    new_x[0] = acc_x[0] + grad
    new_mine[...] = loss_mine[...] + jnp.where(images_are_y, 0.0, loss)
    grad, loss = pair(scalars, other[rows:], y3[...], False)
    new_x[1] = acc_x[1] + grad
    new_other[...] = loss_other[...] + jnp.where(images_are_y, 0.0, loss)


def with_loss(out, grad, loss):
    width = grad.shape[-1]
    out[:, :width] = grad.astype(BF16)
    high = loss.astype(BF16).astype(F32)
    lane = lax.broadcasted_iota(jnp.int32, (grad.shape[0], EXTRA), 1)
    out[:, width:] = jnp.where(lane < EXTRA // 2, high, loss - high).astype(BF16)


def loss_in(block, width):
    high = block[:, width : width + 1].astype(F32)
    low = block[:, width + EXTRA // 2 : width + EXTRA // 2 + 1].astype(F32)
    return high + low


def x3_kernel(
    flags, scalars, mine, other, x3, acc_y, loss_mine, loss_other, out_y, new_mine, new_other, send
):
    rows = x3.shape[0]
    images_are_y = flags[0] == 0
    grad, loss = pair(scalars, other[:rows], x3[...], False)
    total_other = loss_other[...] + jnp.where(images_are_y, loss, 0.0)
    new_other[...] = total_other
    with_loss(send, acc_y[1] + grad, total_other)
    grad, loss = pair(scalars, mine[rows:], x3[...], False)
    out_y[...] = acc_y[0] + grad
    new_mine[...] = loss_mine[...] + jnp.where(images_are_y, loss, 0.0)


def y4_kernel(flags, scalars, other, y4, acc_x, loss_other, send):
    rows = y4.shape[0]
    images_are_y = flags[0] == 0
    grad, loss = pair(scalars, other[rows:], y4[...], False)
    with_loss(send, acc_x[1] + grad, loss_other[...] + jnp.where(images_are_y, 0.0, loss))


def sum_kernel(at, acc, loss, received, send):
    width = acc.shape[-1]
    own = acc[...] if at is None else acc[at]
    block = received[...]
    with_loss(
        send,
        own + block[:, :width].astype(F32),
        loss[...] + loss_in(block, width),
    )


def finish_kernel(
    flags,
    images,
    texts,
    acc_x,
    acc_y,
    loss_mine,
    from_core_x,
    from_core_y,
    home_x,
    home_y,
    loss_out,
    grad_images,
    grad_texts,
):
    width = images.shape[-1]
    stays = flags[0] == flags[1]
    images_are_x = flags[1] == 1

    def write(out, raw, grad):
        unit, inverse = unit_and_inverse(raw[...])
        along = jnp.sum(unit * grad, axis=-1, keepdims=True)
        out[...] = inverse * (grad - unit * along)

    def write_both(grad_x, loss_x, grad_y, loss_y):
        @pl.when(images_are_x)
        def _():
            write(grad_images, images, grad_x())
            write(grad_texts, texts, grad_y())
            loss_out[...] = loss_x()

        @pl.when(jnp.logical_not(images_are_x))
        def _():
            write(grad_images, images, grad_y())
            write(grad_texts, texts, grad_x())
            loss_out[...] = loss_y()

    @pl.when(stays)
    def _():
        write_both(
            lambda: acc_x[0] + from_core_x[:, :width].astype(F32),
            lambda: loss_mine[...] + loss_in(from_core_x, width),
            lambda: acc_y[...] + from_core_y[:, :width].astype(F32),
            lambda: loss_mine[...] + loss_in(from_core_y, width),
        )

    @pl.when(jnp.logical_not(stays))
    def _():
        write_both(
            lambda: home_x[:, :width].astype(F32),
            lambda: loss_in(home_x, width),
            lambda: home_y[:, :width].astype(F32),
            lambda: loss_in(home_y, width),
        )


def call(kernel, outs, n_smem, args):
    return pl.pallas_call(
        kernel,
        out_shape=outs,
        in_specs=smem(n_smem) + vmem(len(args) - n_smem),
        out_specs=vmem(len(outs)),
        compiler_params=pltpu.CompilerParams(vmem_limit_bytes=48 * 1024 * 1024),
        cost_estimate=pl.CostEstimate(flops=1, bytes_accessed=1, transcendentals=0),
    )(*args)


def tied(block, *earlier):
    return lax.optimization_barrier((block, *earlier))[0]


def routes(blks, grps):
    total = blks * grps

    def turned(device):
        blk, grp = divmod(device, grps)
        return (blk - blk % 2 + grp % 2) * grps + grp - grp % 2 + blk % 2

    def step(block, role):
        texts = (block % 2 == 0) == (role == "x")
        return (block + (2 if texts else -2)) % total

    blocks = range(total)
    first = {r: [(b, turned(step(b, r))) for b in blocks] for r in "xy"}
    later = {r: [(turned(b), turned(step(b, r))) for b in blocks] for r in "xy"}
    swap = [(b, turned(b)) for b in blocks]
    home = [(turned(b), b) for b in blocks if turned(b) != b]

    def across(device):
        blk, grp = divmod(device, grps)
        return (blk + 1 - 2 * (blk % 2)) * grps + grp

    cores = [(b, across(b)) for b in blocks]
    return first, later, swap, home, cores


def on_device(images, texts, scale, offset):
    rows, width = images.shape
    blks, grps = lax.axis_size("blk"), lax.axis_size("grp")
    first, later, swap, home, cores = routes(blks, grps)
    flags = jnp.stack([lax.axis_index("blk") % 2, lax.axis_index("grp") % 2]).astype(jnp.int32)
    scalars = jnp.concatenate([scale, offset])
    move = lambda block, route: lax.ppermute(block, AXES, route)

    block = jax.ShapeDtypeStruct((rows, width), BF16)
    wide = jax.ShapeDtypeStruct((rows, width + EXTRA), BF16)
    column = jax.ShapeDtypeStruct((rows, 1), F32)
    total = jax.ShapeDtypeStruct((rows, width), F32)
    totals = jax.ShapeDtypeStruct((2, rows, width), F32)
    work = 4 * rows * rows * width

    x, y, both = call(
        prepare_kernel,
        (block, block, jax.ShapeDtypeStruct((2 * rows, width), BF16)),
        1,
        (flags, images, texts),
    )
    y1 = move(y, first["y"])
    x1 = move(x, first["x"])
    y2 = move(y1, later["y"])
    x2 = move(x1, later["x"])
    mine = move(tied(both, x1, y1), swap)
    other = move(tied(mine, x2, y2), cores)
    y3 = move(y2, later["y"])
    x3 = move(x2, later["x"])

    acc_x, acc_y, loss_mine, loss_other = call(
        early_kernel,
        (totals, totals, column, column),
        2,
        (flags, scalars, mine, other, x1, y1, x2, y2),
    )
    y3 = tied(y3, acc_x)
    y4 = move(y3, later["y"])
    acc_x, loss_mine, loss_other = call(
        y3_kernel,
        (totals, column, column),
        2,
        (flags, scalars, mine, other, y3, acc_x, loss_mine, loss_other),
    )
    x3 = tied(x3, acc_x)
    acc_y, loss_mine, loss_other, send_y = call(
        x3_kernel,
        (total, column, column, wide),
        2,
        (flags, scalars, mine, other, x3, acc_y, loss_mine, loss_other),
    )
    from_core_x = move(send_y, cores)
    (back_x,) = call(
        functools.partial(sum_kernel, 0), (wide,), 0, (acc_x, loss_mine, from_core_x)
    )
    home_x = move(back_x, home)
    y4 = tied(y4, back_x)
    (send_x,) = call(
        y4_kernel,
        (wide,),
        2,
        (flags, scalars, other, y4, acc_x, loss_other),
    )
    from_core_y = move(send_x, cores)
    (back_y,) = call(
        functools.partial(sum_kernel, None), (wide,), 0, (acc_y, loss_mine, from_core_y)
    )
    home_y = move(back_y, home)
    loss, grad_images, grad_texts = call(
        finish_kernel,
        (column, total, total),
        1,
        (
            flags,
            images,
            texts,
            acc_x,
            acc_y,
            loss_mine,
            from_core_x,
            from_core_y,
            home_x,
            home_y,
        ),
    )
    return loss.reshape(rows), grad_images, grad_texts


def solution(mesh):
    return jax.shard_map(
        on_device,
        mesh=mesh,
        in_specs=(P(AXES, None), P(AXES, None), P(), P()),
        out_specs=(P(AXES), P(AXES, None), P(AXES, None)),
        check_vma=False,
    )
```

time: 253 us -> 149 us (0.59); the launches traced: 249 us -> 148 us
  waiting for transfers between devices: 193 us -> 58 us
  starting transfers between devices: 34.7 us -> 60.7 us
  Pallas kernels: 0 us -> 24.2 us
  matrix products: 11.6 us -> 0 us
  other arithmetic: 6.88 us -> 0.83 us
    ppermute x15 -> x13, waiting for transfers between devices: 193 us -> 58 us  [on_device(): move = lambda block, route: lax.ppermute(block, AXES, route)]
    ppermute x15 -> x13, starting transfers between devices: 34.7 us -> 60.7 us  [on_device(): move = lambda block, route: lax.ppermute(block, AXES, route)]
    pallas_call x0 -> x8, Pallas kernels: none -> 24.2 us  [call(): pl.pallas_call(kernel, out_shape=outs, in_specs=smem(n_smem) + vmem(len(a...]
    dot_general x24 -> x0, matrix products: 11.6 us -> none  [the longest x8 4.69 us: pairwise_loss_terms(): lax.dot_general(image_block_rows, text_block_rows, (((1,), (1,)), ((), ()...]
    mul x2 -> x0, other arithmetic: 2.58 us -> none  [back_norm(): return inverse * (grad_unit - unit32 * along)]
  transfers between devices with their start and end apart: 15 -> 13, of which waited for: 15 -> 8; matrix products, arithmetic and copies ran while one was open for 6% -> 0% of each run, Pallas kernels for 0% -> 9%
where the time goes in v1:
time: 149 us; the launch traced here: 148 us
  starting transfers between devices  60.7 us (41%)
  waiting for transfers between devices  58 us (39%)
  Pallas kernels  24.2 us (16%)
  between operations  2.16 us (1%)
  local copies, waits for them, and re-layouts  2.14 us (1%)
    ppermute x13, starting transfers between devices, on_device(): move = lambda block, route: lax.ppermute(block, AXES, route)  60.7 us
    ppermute x13, waiting for transfers between devices, on_device(): move = lambda block, route: lax.ppermute(block, AXES, route)  58 us
    pallas_call x8, Pallas kernels, call(): pl.pallas_call(kernel, out_shape=outs, in_specs=smem(n_smem) + vmem(len(a...  24.2 us
  transfers between devices with their start and end apart: 13, of which 8 were waited for; matrix products, arithmetic and copies ran while one was open for 0% of the time, Pallas kernels for 9%

profile of v1, /device:TPU:1, one launch (start us, length us, event | category | flops | bytes accessed | tf_op | source)
XLA Modules:
  0.0 148.1 jit_solution(2463575761174941763)
XLA Ops:
  0.7 0.1 pad_add_fusion.flags
  0.7 0.0 copy-start.1
  0.7 1.1 copy-done.1
  1.8 0.0 copy-start.3
  1.8 1.1 copy-done.3
  2.9 1.1 shard_map.67
  4.0 6.4 %collective-permute-start = (bf16[256,1152]{1,0:T(8,128)(2,1)S(1)}, bf16[256,1152]{1,0:T(8,128)(2,1)S(1)}, u32[]{:S(2)}, u32[]{:S(2)}) collective-permute-start(bf16[256,1152]{1,0:T(8,128)(2,1)S(1)} %get-tuple-element.26), channel_id=1, source_target_pairs={{0,2},{1,767},{2,4},{3,24},{4,6},{5,26},{6,8},{7,28},{8,10},{9,30}... | collective-permute-start | bytes 1769480 | tf_op jit(solution)/shard_map/ppermute | solution.py:267
  10.4 11.2 %collective-permute-start.1 = (bf16[256,1152]{1,0:T(8,128)(2,1)S(1)}, bf16[256,1152]{1,0:T(8,128)(2,1)S(1)}, u32[]{:S(2)}, u32[]{:S(2)}) collective-permute-start(bf16[256,1152]{1,0:T(8,128)(2,1)S(1)} %get-tuple-element.27), channel_id=1, source_target_pairs={{0,743},{1,26},{2,0},{3,28},{4,2},{5,30},{6,4},{7,32},{8,6},{9,34}... | collective-permute-start | bytes 1769480 | tf_op jit(solution)/shard_map/ppermute | solution.py:267
  21.6 1.9 %collective-permute-done.x1 = bf16[256,1152]{1,0:T(8,128)(2,1)S(1)} collective-permute-done((bf16[256,1152]{1,0:T(8,128)(2,1)S(1)}, bf16[256,1152]{1,0:T(8,128)(2,1)S(1)}, u32[]{:S(2)}, u32[]{:S(2)}) %collective-permute-start) | collective-permute-done | bytes 589856 | tf_op jit(solution)/shard_map/ppermute | solution.py:267
  23.6 13.9 %collective-permute-done.1.y1 = bf16[256,1152]{1,0:T(8,128)(2,1)S(1)} collective-permute-done((bf16[256,1152]{1,0:T(8,128)(2,1)S(1)}, bf16[256,1152]{1,0:T(8,128)(2,1)S(1)}, u32[]{:S(2)}, u32[]{:S(2)}) %collective-permute-start.1) | collective-permute-done | bytes 589856 | tf_op jit(solution)/shard_map/ppermute | solution.py:267
  37.5 4.3 %collective-permute-start.2 = (bf16[512,1152]{1,0:T(8,128)(2,1)S(1)}, bf16[512,1152]{1,0:T(8,128)(2,1)S(1)}, u32[]{:S(2)}, u32[]{:S(2)}) collective-permute-start(bf16[512,1152]{1,0:T(8,128)(2,1)S(1)} %get-tuple-element.28), channel_id=1, source_target_pairs={{0,0},{1,24},{2,2},{3,26},{4,4},{5,28},{6,6},{7,30},{8,8},{9,32},{... | collective-permute-start | bytes 3538952 | tf_op jit(solution)/shard_map/ppermute | solution.py:267
  41.8 9.1 %collective-permute-start.3 = (bf16[256,1152]{1,0:T(8,128)(2,1)S(1)}, bf16[256,1152]{1,0:T(8,128)(2,1)S(1)}, u32[]{:S(2)}, u32[]{:S(2)}) collective-permute-start(bf16[256,1152]{1,0:T(8,128)(2,1)S(1)} %collective-permute-done.x1), channel_id=1, source_target_pairs={{0,2},{24,767},{2,4},{26,24},{4,6},{28,26},{6,8},{30,28},{8,10},{3... | collective-permute-start | bytes 1769480 | tf_op jit(solution)/shard_map/ppermute | solution.py:267
  50.9 1.9 %collective-permute-start.4 = (bf16[256,1152]{1,0:T(8,128)(2,1)S(1)}, bf16[256,1152]{1,0:T(8,128)(2,1)S(1)}, u32[]{:S(2)}, u32[]{:S(2)}) collective-permute-start(bf16[256,1152]{1,0:T(8,128)(2,1)S(1)} %collective-permute-done.1.y1), channel_id=1, source_target_pairs={{0,743},{24,26},{2,0},{26,28},{4,2},{28,30},{6,4},{30,32},{8,6},{3... | collective-permute-start | bytes 1769480 | tf_op jit(solution)/shard_map/ppermute | solution.py:267
  52.8 6.0 %collective-permute-done.3.x2 = bf16[256,1152]{1,0:T(8,128)(2,1)S(1)} collective-permute-done((bf16[256,1152]{1,0:T(8,128)(2,1)S(1)}, bf16[256,1152]{1,0:T(8,128)(2,1)S(1)}, u32[]{:S(2)}, u32[]{:S(2)}) %collective-permute-start.3) | collective-permute-done | bytes 589856 | tf_op jit(solution)/shard_map/ppermute | solution.py:267
  58.9 8.6 %collective-permute-done.4.y2 = bf16[256,1152]{1,0:T(8,128)(2,1)S(1)} collective-permute-done((bf16[256,1152]{1,0:T(8,128)(2,1)S(1)}, bf16[256,1152]{1,0:T(8,128)(2,1)S(1)}, u32[]{:S(2)}, u32[]{:S(2)}) %collective-permute-start.4) | collective-permute-done | bytes 589856 | tf_op jit(solution)/shard_map/ppermute | solution.py:267
  67.4 0.9 collective-permute-done.2.mine
  68.3 1.9 %collective-permute-start.5 = (bf16[512,1152]{1,0:T(8,128)(2,1)S(1)}, bf16[512,1152]{1,0:T(8,128)(2,1)S(1)}, u32[]{:S(2)}, u32[]{:S(2)}) collective-permute-start(bf16[512,1152]{1,0:T(8,128)(2,1)S(1)} %collective-permute-done.2.mine), channel_id=1, source_target_pairs={{0,24},{1,25},{2,26},{3,27},{4,28},{5,29},{6,30},{7,31},{8,32},{9,... | collective-permute-start | bytes 3538952 | tf_op jit(solution)/shard_map/ppermute | solution.py:267
  70.2 1.9 %collective-permute-start.6 = (bf16[256,1152]{1,0:T(8,128)(2,1)S(1)}, bf16[256,1152]{1,0:T(8,128)(2,1)S(1)}, u32[]{:S(2)}, u32[]{:S(2)}) collective-permute-start(bf16[256,1152]{1,0:T(8,128)(2,1)S(1)} %collective-permute-done.4.y2), channel_id=1, source_target_pairs={{0,743},{24,26},{2,0},{26,28},{4,2},{28,30},{6,4},{30,32},{8,6},{3... | collective-permute-start | bytes 1769480 | tf_op jit(solution)/shard_map/ppermute | solution.py:267
  72.1 11.0 %collective-permute-start.7 = (bf16[256,1152]{1,0:T(8,128)(2,1)S(1)}, bf16[256,1152]{1,0:T(8,128)(2,1)S(1)}, u32[]{:S(2)}, u32[]{:S(2)}) collective-permute-start(bf16[256,1152]{1,0:T(8,128)(2,1)S(1)} %collective-permute-done.3.x2), channel_id=1, source_target_pairs={{0,2},{24,767},{2,4},{26,24},{4,6},{28,26},{6,8},{30,28},{8,10},{3... | collective-permute-start | bytes 1769480 | tf_op jit(solution)/shard_map/ppermute | solution.py:267
  84.5 0.1 pad_maximum_fusion.scalars
  84.6 0.0 collective-permute-done.5.other
  84.6 8.7 %shard_map.68 = (f32[2,256,1152]{2,1,0:T(8,128)}, f32[2,256,1152]{2,1,0:T(8,128)}, f32[256,1]{1,0:T(8,128)S(1)}, f32[256,1]{1,0:T(8,128)S(1)}) custom-call(s32[2]{0:T(128)S(1)} %pad_add_fusion.flags, f32[2]{0:T(128)S(1)} %pad_maximum_fusion.scalars, bf16[512,1152]{1,0:T(8,128)(2,1)S(1)} %collective-permute-done.2.mine, ...), custom_call_target="tpu_custom_call" | custom-call | flops 1 | bytes 1 | tf_op jit(solution)/shard_map/pallas_call | solution.py:222
  93.3 0.0 collective-permute-done.6.y3
  93.3 3.6 %shard_map.69 = (f32[2,256,1152]{2,1,0:T(8,128)S(1)}, f32[256,1]{1,0:T(8,128)S(1)}, f32[256,1]{1,0:T(8,128)S(1)}) custom-call(s32[2]{0:T(128)S(1)} %pad_add_fusion.flags, f32[2]{0:T(128)S(1)} %pad_maximum_fusion.scalars, bf16[512,1152]{1,0:T(8,128)(2,1)S(1)} %collective-permute-done.2.mine, bf16[512,1152]{1,0:T(8,128)(2,1)S(1)} %collective-permute-done.5.other, ...), custom_call_target="tpu_custom_call" | custom-call | flops 1 | bytes 1 | tf_op jit(solution)/shard_map/pallas_call | solution.py:222
  96.9 0.0 copy-start
  96.9 0.0 collective-permute-done.7.x3
  96.9 4.5 %shard_map.70 = (f32[256,1152]{1,0:T(8,128)S(1)}, f32[256,1]{1,0:T(8,128)S(1)}, f32[256,1]{1,0:T(8,128)S(1)}, bf16[256,1280]{1,0:T(8,128)(2,1)S(1)}) custom-call(s32[2]{0:T(128)S(1)} %pad_add_fusion.flags, f32[2]{0:T(128)S(1)} %pad_maximum_fusion.scalars, bf16[512,1152]{1,0:T(8,128)(2,1)S(1)} %collective-permute-done.2.mine, ...), custom_call_target="tpu_custom_call" | custom-call | flops 1 | bytes 1 | tf_op jit(solution)/shard_map/pallas_call | solution.py:222
  101.4 2.9 %collective-permute-start.8 = (bf16[256,1280]{1,0:T(8,128)(2,1)S(1)}, bf16[256,1280]{1,0:T(8,128)(2,1)S(1)}, u32[]{:S(2)}, u32[]{:S(2)}) collective-permute-start(bf16[256,1280]{1,0:T(8,128)(2,1)S(1)} %get-tuple-element.41), channel_id=1, source_target_pairs={{0,24},{1,25},{2,26},{3,27},{4,28},{5,29},{6,30},{7,31},{8,32},{9,... | collective-permute-start | bytes 1966088 | tf_op jit(solution)/shard_map/ppermute | solution.py:267
  104.3 1.9 %collective-permute-start.9 = (bf16[256,1152]{1,0:T(8,128)(2,1)S(1)}, bf16[256,1152]{1,0:T(8,128)(2,1)S(1)}, u32[]{:S(2)}, u32[]{:S(2)}) collective-permute-start(bf16[256,1152]{1,0:T(8,128)(2,1)S(1)} %collective-permute-done.6.y3), channel_id=1, source_target_pairs={{0,743},{24,26},{2,0},{26,28},{4,2},{28,30},{6,4},{30,32},{8,6},{3... | collective-permute-start | bytes 1769480 | tf_op jit(solution)/shard_map/ppermute | solution.py:267
  106.2 0.0 collective-permute-done.8.received.from_core_x
  106.2 0.4 shard_map.71
  106.6 13.9 %collective-permute-done.9.y4 = bf16[256,1152]{1,0:T(8,128)(2,1)S(1)} collective-permute-done((bf16[256,1152]{1,0:T(8,128)(2,1)S(1)}, bf16[256,1152]{1,0:T(8,128)(2,1)S(1)}, u32[]{:S(2)}, u32[]{:S(2)}) %collective-permute-start.9) | collective-permute-done | bytes 589856 | tf_op jit(solution)/shard_map/ppermute | solution.py:267
  120.6 0.0 copy-done
  120.6 1.6 %shard_map.72 = bf16[256,1280]{1,0:T(8,128)(2,1)S(1)} custom-call(s32[2]{0:T(128)S(1)} %pad_add_fusion.flags, f32[2]{0:T(128)S(1)} %pad_maximum_fusion.scalars, bf16[512,1152]{1,0:T(8,128)(2,1)S(1)} %collective-permute-done.5.other, bf16[256,1152]{1,0:T(8,128)(2,1)S(1)} %collective-permute-done.9.y4, f32[2,256,1152]{2,1,0:T(8,128)S(1)} %get-tuple-element.34.acc.acc_x, ...), custom_call_target="tpu_custom_call" | custom-call | flops 1 | bytes 1 | tf_op jit(solution)/shard_map/pallas_call | solution.py:222
  122.2 2.3 %collective-permute-start.10 = (bf16[256,1280]{1,0:T(8,128)(2,1)S(1)}, bf16[256,1280]{1,0:T(8,128)(2,1)S(1)}, u32[]{:S(2)}, u32[]{:S(2)}) collective-permute-start(bf16[256,1280]{1,0:T(8,128)(2,1)S(1)} %shard_map.72), channel_id=1, source_target_pairs={{0,24},{1,25},{2,26},{3,27},{4,28},{5,29},{6,30},{7,31},{8,32},{9,... | collective-permute-start | bytes 1966088 | tf_op jit(solution)/shard_map/ppermute | solution.py:267
  124.5 2.1 %collective-permute-start.11 = (bf16[256,1280]{1,0:T(8,128)(2,1)S(1)}, bf16[256,1280]{1,0:T(8,128)(2,1)S(1)}, u32[]{:S(2)}, u32[]{:S(2)}) collective-permute-start(bf16[256,1280]{1,0:T(8,128)(2,1)S(1)} %shard_map.71), channel_id=1, source_target_pairs={{24,1},{26,3},{28,5},{30,7},{32,9},{34,11},{36,13},{38,15},{40,17}... | collective-permute-start | bytes 1966088 | tf_op jit(solution)/shard_map/ppermute | solution.py:267
  126.6 0.0 collective-permute-done.10.received.from_core_y
  126.6 0.0 copy-start.2
  126.7 0.0 copy-start.4
  126.7 0.4 shard_map.73
  127.0 3.6 %collective-permute-start.12 = (bf16[256,1280]{1,0:T(8,128)(2,1)S(1)}, bf16[256,1280]{1,0:T(8,128)(2,1)S(1)}, u32[]{:S(2)}, u32[]{:S(2)}) collective-permute-start(bf16[256,1280]{1,0:T(8,128)(2,1)S(1)} %shard_map.73), channel_id=1, source_target_pairs={{24,1},{26,3},{28,5},{30,7},{32,9},{34,11},{36,13},{38,15},{40,17}... | collective-permute-start | bytes 1966088 | tf_op jit(solution)/shard_map/ppermute | solution.py:267
  130.7 5.8 %collective-permute-done.11.home_x = bf16[256,1280]{1,0:T(8,128)(2,1)S(1)} collective-permute-done((bf16[256,1280]{1,0:T(8,128)(2,1)S(1)}, bf16[256,1280]{1,0:T(8,128)(2,1)S(1)}, u32[]{:S(2)}, u32[]{:S(2)}) %collective-permute-start.11) | collective-permute-done | bytes 655392 | tf_op jit(solution)/shard_map/ppermute | solution.py:267
  136.4 7.0 %collective-permute-done.12.home_y = bf16[256,1280]{1,0:T(8,128)(2,1)S(1)} collective-permute-done((bf16[256,1280]{1,0:T(8,128)(2,1)S(1)}, bf16[256,1280]{1,0:T(8,128)(2,1)S(1)}, u32[]{:S(2)}, u32[]{:S(2)}) %collective-permute-start.12) | collective-permute-done | bytes 655392 | tf_op jit(solution)/shard_map/ppermute | solution.py:267
  143.4 0.0 copy-done.2
  143.5 0.0 copy-done.4
  143.5 4.0 %shard_map.74 = (f32[256,1]{1,0:T(8,128)S(1)}, f32[256,1152]{1,0:T(8,128)}, f32[256,1152]{1,0:T(8,128)}) custom-call(s32[2]{0:T(128)S(1)} %pad_add_fusion.flags, bf16[256,1152]{1,0:T(8,128)(2,1)S(1)} %copy-done.2, bf16[256,1152]{1,0:T(8,128)(2,1)S(1)} %copy-done.4, f32[2,256,1152]{2,1,0:T(8,128)} %copy-done, f32[256,1152]{1,0:T(8,128)S(1)} %get-tuple-element.39.acc.acc_y, ...), custom_call_target="tpu_custom_call" | custom-call | flops 1 | bytes 1 | tf_op jit(solution)/shard_map/pallas_call | solution.py:222
  147.5 0.7 reduce
Async XLA Ops:
  0.7 1.1 copy-start.1
  1.8 1.1 copy-start.3
  4.0 19.6 %collective-permute-start = (bf16[256,1152]{1,0:T(8,128)(2,1)S(1)}, bf16[256,1152]{1,0:T(8,128)(2,1)S(1)}, u32[]{:S(2)}, u32[]{:S(2)}) collective-permute-start(bf16[256,1152]{1,0:T(8,128)(2,1)S(1)} %get-tuple-element.26), channel_id=1, source_target_pairs={{0,2},{1,767},{2,4},{3,24},{4,6},{5,26},{6,8},{7,28},{8,10},{9,30}... | collective-permute-start | bytes 1769480 | tf_op jit(solution)/shard_map/ppermute | solution.py:267
  10.4 27.1 %collective-permute-start.1 = (bf16[256,1152]{1,0:T(8,128)(2,1)S(1)}, bf16[256,1152]{1,0:T(8,128)(2,1)S(1)}, u32[]{:S(2)}, u32[]{:S(2)}) collective-permute-start(bf16[256,1152]{1,0:T(8,128)(2,1)S(1)} %get-tuple-element.27), channel_id=1, source_target_pairs={{0,743},{1,26},{2,0},{3,28},{4,2},{5,30},{6,4},{7,32},{8,6},{9,34}... | collective-permute-start | bytes 1769480 | tf_op jit(solution)/shard_map/ppermute | solution.py:267
  37.5 30.8 %collective-permute-start.2 = (bf16[512,1152]{1,0:T(8,128)(2,1)S(1)}, bf16[512,1152]{1,0:T(8,128)(2,1)S(1)}, u32[]{:S(2)}, u32[]{:S(2)}) collective-permute-start(bf16[512,1152]{1,0:T(8,128)(2,1)S(1)} %get-tuple-element.28), channel_id=1, source_target_pairs={{0,0},{1,24},{2,2},{3,26},{4,4},{5,28},{6,6},{7,30},{8,8},{9,32},{... | collective-permute-start | bytes 3538952 | tf_op jit(solution)/shard_map/ppermute | solution.py:267
  41.8 17.1 %collective-permute-start.3 = (bf16[256,1152]{1,0:T(8,128)(2,1)S(1)}, bf16[256,1152]{1,0:T(8,128)(2,1)S(1)}, u32[]{:S(2)}, u32[]{:S(2)}) collective-permute-start(bf16[256,1152]{1,0:T(8,128)(2,1)S(1)} %collective-permute-done.x1), channel_id=1, source_target_pairs={{0,2},{24,767},{2,4},{26,24},{4,6},{28,26},{6,8},{30,28},{8,10},{3... | collective-permute-start | bytes 1769480 | tf_op jit(solution)/shard_map/ppermute | solution.py:267
  50.9 16.5 %collective-permute-start.4 = (bf16[256,1152]{1,0:T(8,128)(2,1)S(1)}, bf16[256,1152]{1,0:T(8,128)(2,1)S(1)}, u32[]{:S(2)}, u32[]{:S(2)}) collective-permute-start(bf16[256,1152]{1,0:T(8,128)(2,1)S(1)} %collective-permute-done.1.y1), channel_id=1, source_target_pairs={{0,743},{24,26},{2,0},{26,28},{4,2},{28,30},{6,4},{30,32},{8,6},{3... | collective-permute-start | bytes 1769480 | tf_op jit(solution)/shard_map/ppermute | solution.py:267
  68.3 16.3 %collective-permute-start.5 = (bf16[512,1152]{1,0:T(8,128)(2,1)S(1)}, bf16[512,1152]{1,0:T(8,128)(2,1)S(1)}, u32[]{:S(2)}, u32[]{:S(2)}) collective-permute-start(bf16[512,1152]{1,0:T(8,128)(2,1)S(1)} %collective-permute-done.2.mine), channel_id=1, source_target_pairs={{0,24},{1,25},{2,26},{3,27},{4,28},{5,29},{6,30},{7,31},{8,32},{9,... | collective-permute-start | bytes 3538952 | tf_op jit(solution)/shard_map/ppermute | solution.py:267
  70.2 23.1 %collective-permute-start.6 = (bf16[256,1152]{1,0:T(8,128)(2,1)S(1)}, bf16[256,1152]{1,0:T(8,128)(2,1)S(1)}, u32[]{:S(2)}, u32[]{:S(2)}) collective-permute-start(bf16[256,1152]{1,0:T(8,128)(2,1)S(1)} %collective-permute-done.4.y2), channel_id=1, source_target_pairs={{0,743},{24,26},{2,0},{26,28},{4,2},{28,30},{6,4},{30,32},{8,6},{3... | collective-permute-start | bytes 1769480 | tf_op jit(solution)/shard_map/ppermute | solution.py:267
  72.1 24.7 %collective-permute-start.7 = (bf16[256,1152]{1,0:T(8,128)(2,1)S(1)}, bf16[256,1152]{1,0:T(8,128)(2,1)S(1)}, u32[]{:S(2)}, u32[]{:S(2)}) collective-permute-start(bf16[256,1152]{1,0:T(8,128)(2,1)S(1)} %collective-permute-done.3.x2), channel_id=1, source_target_pairs={{0,2},{24,767},{2,4},{26,24},{4,6},{28,26},{6,8},{30,28},{8,10},{3... | collective-permute-start | bytes 1769480 | tf_op jit(solution)/shard_map/ppermute | solution.py:267
  96.9 23.7 %copy-start = (f32[2,256,1152]{2,1,0:T(8,128)}, f32[2,256,1152]{2,1,0:T(8,128)S(1)}, u32[]{:S(2)}) copy-start(f32[2,256,1152]{2,1,0:T(8,128)S(1)} %get-tuple-element.34.acc.acc_x) | copy-start | bytes 7077892
  101.4 4.9 %collective-permute-start.8 = (bf16[256,1280]{1,0:T(8,128)(2,1)S(1)}, bf16[256,1280]{1,0:T(8,128)(2,1)S(1)}, u32[]{:S(2)}, u32[]{:S(2)}) collective-permute-start(bf16[256,1280]{1,0:T(8,128)(2,1)S(1)} %get-tuple-element.41), channel_id=1, source_target_pairs={{0,24},{1,25},{2,26},{3,27},{4,28},{5,29},{6,30},{7,31},{8,32},{9,... | collective-permute-start | bytes 1966088 | tf_op jit(solution)/shard_map/ppermute | solution.py:267
  104.3 16.2 %collective-permute-start.9 = (bf16[256,1152]{1,0:T(8,128)(2,1)S(1)}, bf16[256,1152]{1,0:T(8,128)(2,1)S(1)}, u32[]{:S(2)}, u32[]{:S(2)}) collective-permute-start(bf16[256,1152]{1,0:T(8,128)(2,1)S(1)} %collective-permute-done.6.y3), channel_id=1, source_target_pairs={{0,743},{24,26},{2,0},{26,28},{4,2},{28,30},{6,4},{30,32},{8,6},{3... | collective-permute-start | bytes 1769480 | tf_op jit(solution)/shard_map/ppermute | solution.py:267
  122.2 4.4 %collective-permute-start.10 = (bf16[256,1280]{1,0:T(8,128)(2,1)S(1)}, bf16[256,1280]{1,0:T(8,128)(2,1)S(1)}, u32[]{:S(2)}, u32[]{:S(2)}) collective-permute-start(bf16[256,1280]{1,0:T(8,128)(2,1)S(1)} %shard_map.72), channel_id=1, source_target_pairs={{0,24},{1,25},{2,26},{3,27},{4,28},{5,29},{6,30},{7,31},{8,32},{9,... | collective-permute-start | bytes 1966088 | tf_op jit(solution)/shard_map/ppermute | solution.py:267
  124.5 11.9 %collective-permute-start.11 = (bf16[256,1280]{1,0:T(8,128)(2,1)S(1)}, bf16[256,1280]{1,0:T(8,128)(2,1)S(1)}, u32[]{:S(2)}, u32[]{:S(2)}) collective-permute-start(bf16[256,1280]{1,0:T(8,128)(2,1)S(1)} %shard_map.71), channel_id=1, source_target_pairs={{24,1},{26,3},{28,5},{30,7},{32,9},{34,11},{36,13},{38,15},{40,17}... | collective-permute-start | bytes 1966088 | tf_op jit(solution)/shard_map/ppermute | solution.py:267
  126.6 16.8 %copy-start.2 = (bf16[256,1152]{1,0:T(8,128)(2,1)S(1)}, bf16[256,1152]{1,0:T(8,128)(2,1)}, u32[]{:S(2)}) copy-start(bf16[256,1152]{1,0:T(8,128)(2,1)} %images.3) | copy-start | bytes 1769476
  126.7 16.8 %copy-start.4 = (bf16[256,1152]{1,0:T(8,128)(2,1)S(1)}, bf16[256,1152]{1,0:T(8,128)(2,1)}, u32[]{:S(2)}) copy-start(bf16[256,1152]{1,0:T(8,128)(2,1)} %texts.3) | copy-start | bytes 1769476
  127.0 16.4 %collective-permute-start.12 = (bf16[256,1280]{1,0:T(8,128)(2,1)S(1)}, bf16[256,1280]{1,0:T(8,128)(2,1)S(1)}, u32[]{:S(2)}, u32[]{:S(2)}) collective-permute-start(bf16[256,1280]{1,0:T(8,128)(2,1)S(1)} %shard_map.73), channel_id=1, source_target_pairs={{24,1},{26,3},{28,5},{30,7},{32,9},{34,11},{36,13},{38,15},{40,17}... | collective-permute-start | bytes 1966088 | tf_op jit(solution)/shard_map/ppermute | solution.py:267

commit v2 on v0

v2 whole, which is shorter than its diff:
```python
import functools

import jax
import jax.numpy as jnp
from jax import lax
from jax.experimental import pallas as pl
from jax.experimental.pallas import tpu as pltpu
from jax.sharding import PartitionSpec as P

AXES = ("blk", "grp")
BF16 = jnp.bfloat16
F32 = jnp.float32
EXTRA = 128
PIECES = 4
LAST = 288


def vmem(count):
    return [pl.BlockSpec(memory_space=pltpu.VMEM)] * count


def smem(count):
    return [pl.BlockSpec(memory_space=pltpu.SMEM)] * count


def unit_and_inverse(raw):
    wide = raw.astype(F32)
    inverse = lax.rsqrt(jnp.sum(wide * wide, axis=-1, keepdims=True) + 1e-06)
    return wide * inverse, inverse


def prepare_kernel(flags, images, texts, both):
    rows = images.shape[0]
    img = unit_and_inverse(images[...])[0].astype(BF16)
    txt = unit_and_inverse(texts[...])[0].astype(BF16)
    even = flags[1] == 0

    @pl.when(even)
    def _():
        both[:rows] = txt
        both[rows:] = img

    @pl.when(jnp.logical_not(even))
    def _():
        both[:rows] = img
        both[rows:] = txt


def stack_kernel(second, first, stacked):
    rows = first.shape[0]
    stacked[:rows] = unit_and_inverse(first[...])[0].astype(BF16)
    stacked[rows:] = unit_and_inverse(second[...])[0].astype(BF16)


def joined(a, b):
    return a + b + a * b


def pair(scalars, rows, columns, diagonal=False):
    scale, offset = scalars[0], scalars[1]
    logits = (
        scale
        * lax.dot_general(rows, columns, (((1,), (1,)), ((), ())), preferred_element_type=F32)
        + offset
    )
    if diagonal:
        i = lax.broadcasted_iota(jnp.int32, logits.shape, 0)
        j = lax.broadcasted_iota(jnp.int32, logits.shape, 1)
        negated = jnp.where(i == j, -1.0, 1.0).astype(F32)
        logits = negated * logits
    small = jnp.exp(-jnp.abs(logits))
    share = scale / (1.0 + small)
    weights = jnp.where(logits >= 0, share, small * share)
    if diagonal:
        weights = negated * weights
    above = jnp.maximum(logits, 0.0)
    half = logits.shape[1] // 2
    return (
        jnp.dot(weights.astype(BF16), columns, preferred_element_type=F32),
        above[:, :half] + above[:, half:],
        joined(small[:, :half], small[:, half:]),
    )


def side(scalars, rows, columns):
    total = None
    for block, diagonal in columns:
        grad, above, small = pair(scalars, rows, block[...], diagonal)
        if total is None:
            total, total_above, total_small = grad, above, small
        else:
            total = total + grad
            total_above = total_above + above
            total_small = joined(total_small, small)
    return total, total_above, total_small


def early_kernel(scalars, mine, other, pair1, pair2, acc, above, small):
    rows = mine.shape[0] // 2
    later = [(c.at[at : at + rows], False) for c in (pair1, pair2) for at in (0, rows)]
    first, second = (other.at[rows:], True), (mine.at[:rows], True)
    acc[0], above[0], small[0] = side(
        scalars, other[:rows], [first, (mine.at[:rows], False)] + later
    )
    acc[1], above[1], small[1] = side(scalars, mine[rows:], [second] + later)


def with_loss(out, grad, loss):
    width = grad.shape[-1]
    out[:, :width] = grad.astype(BF16)
    high = loss.astype(BF16).astype(F32)
    lane = lax.broadcasted_iota(jnp.int32, (grad.shape[0], EXTRA), 1)
    out[:, width:] = jnp.where(lane < EXTRA // 2, high, loss - high).astype(BF16)


def loss_of(above, small):
    return jnp.sum(above + jnp.log1p(small), axis=-1, keepdims=True)


def loss_in(block, width):
    high = block[:, width : width + 1].astype(F32)
    low = block[:, width + EXTRA // 2 : width + EXTRA // 2 + 1].astype(F32)
    return high + low


def third_first_kernel(scalars, other, pair3, acc, above, small, send):
    rows = other.shape[0] // 2
    grad, more_above, more_small = side(
        scalars, other[:rows], [(pair3.at[:rows], False), (pair3.at[rows:], False)]
    )
    with_loss(send, acc[0] + grad, loss_of(above[0] + more_above, joined(small[0], more_small)))


def third_second_kernel(scalars, mine, pair3, acc, above, small, new_acc, new_above, new_small):
    rows = mine.shape[0] // 2
    grad, more_above, more_small = side(
        scalars, mine[rows:], [(pair3.at[:rows], False), (pair3.at[rows:], False)]
    )
    new_acc[...] = acc[1] + grad
    new_above[...] = above[1] + more_above
    new_small[...] = joined(small[1], more_small)


def fourth_kernel(scalars, mine, last, acc, above, small, send):
    rows = mine.shape[0] // 2
    grad, more_above, more_small = side(scalars, mine[rows:], [(last.at[:rows], False)])
    with_loss(
        send, acc[...] + grad, loss_of(above[...] + more_above, joined(small[...], more_small))
    )


def as_row(column):
    count = column.shape[0]
    i = lax.broadcasted_iota(jnp.int32, (count, count), 0)
    j = lax.broadcasted_iota(jnp.int32, (count, count), 1)
    return jnp.sum(jnp.where(i == j, column, 0.0), axis=0, keepdims=True)


def back_norm(raw, grad):
    unit, inverse = unit_and_inverse(raw)
    along = jnp.sum(unit * grad, axis=-1, keepdims=True)
    return inverse * (grad - unit * along)


def write_grad(is_image, images, texts, block, grad_images, grad_texts, buf, sem):
    rows, width = images.shape
    count = rows // PIECES

    def copies(out):
        return [
            pltpu.make_async_copy(
                buf.at[at * count : (at + 1) * count],
                out.at[at * count : (at + 1) * count],
                sem.at[at],
            )
            for at in range(PIECES)
        ]

    def write(raw, out):
        for at, copy in enumerate(copies(out)):
            part = slice(at * count, (at + 1) * count)
            buf[part] = back_norm(raw[part], block[part, :width].astype(F32))
            copy.start()
        for copy in copies(out):
            copy.wait()

    pl.when(is_image)(lambda: write(images, grad_images))
    pl.when(jnp.logical_not(is_image))(lambda: write(texts, grad_texts))


def finish_first_kernel(flags, images, texts, block, grad_images, grad_texts, loss, buf, sem):
    loss[...] = as_row(loss_in(block, images.shape[1]))
    write_grad(flags[1] == 1, images, texts, block, grad_images, grad_texts, buf, sem)


def finish_second_kernel(
    flags,
    images,
    texts,
    block,
    loss_first,
    images_so_far,
    texts_so_far,
    grad_images,
    grad_texts,
    loss,
    buf,
    sem,
):
    loss[...] = jnp.where(
        flags[1] == 1, loss_first[...], as_row(loss_in(block, images.shape[1]))
    )
    write_grad(flags[1] == 0, images, texts, block, grad_images, grad_texts, buf, sem)


def call(kernel, outs, n_smem, args, in_hbm=0, outs_hbm=0, scratch=(), aliases=None, us=0.0):
    hbm = lambda count: [pl.BlockSpec(memory_space=pl.ANY)] * count
    return pl.pallas_call(
        kernel,
        out_shape=outs,
        in_specs=smem(n_smem) + vmem(len(args) - n_smem - in_hbm) + hbm(in_hbm),
        out_specs=tuple(hbm(outs_hbm) + vmem(len(outs) - outs_hbm)),
        scratch_shapes=list(scratch),
        input_output_aliases=aliases or {},
        compiler_params=pltpu.CompilerParams(vmem_limit_bytes=24 * 1024 * 1024),
        cost_estimate=pl.CostEstimate(
            flops=1, bytes_accessed=1 + int(us * 3.7e6), transcendentals=0
        ),
    )(*args)


def tied(block, *earlier):
    return lax.optimization_barrier((block, *earlier))[0]


def routes(blks, grps):
    total = blks * grps

    def held_at(block):
        blk, grp = divmod(block, grps)
        turns = blk // 2 % 4 != 3
        column = (blk + (turns and grp >= grps // 2)) % 2
        return blk - blk % 2, grp - grp % 2 + column

    def on_core(block, core):
        blk, grp = held_at(block)
        return (blk + core) * grps + grp

    blocks = range(total)
    ahead = lambda b: (b + 2) % total
    behind = lambda b: (b - 2) % total
    even = [b for b in blocks if b % 2 == 0]
    odd = [b for b in blocks if b % 2 == 1]
    first_x = [(b, on_core(ahead(b), 0)) for b in even] + [(b, on_core(behind(b), 1)) for b in odd]
    first_y = [(b, on_core(behind(b), 1)) for b in even] + [(b, on_core(ahead(b), 0)) for b in odd]
    later = [(on_core(b, 0), on_core(ahead(b), 0)) for b in even]
    later += [(on_core(b, 1), on_core(behind(b), 1)) for b in even]
    swap = [(b, on_core(b, b % 2)) for b in blocks]
    cores = [(on_core(b, b % 2), on_core(b, 1 - b % 2)) for b in blocks]
    home_first = [(on_core(b, 0), b) for b in odd] + [(on_core(b, 1), b) for b in even]
    home_second = [(on_core(b, 0), b) for b in even] + [(on_core(b, 1), b) for b in odd]
    return first_x, first_y, later, swap, cores, home_first, home_second


def on_device(images, texts, scale, offset):
    rows, width = images.shape
    blks, grps = lax.axis_size("blk"), lax.axis_size("grp")
    first_x, first_y, later, swap, cores, home_first, home_second = routes(blks, grps)
    flags = jnp.stack([lax.axis_index("blk") % 2, lax.axis_index("grp") % 2]).astype(jnp.int32)
    scalars = jnp.concatenate([scale, offset])
    move = lambda block, route: lax.ppermute(block, AXES, route)

    double = jax.ShapeDtypeStruct((2 * rows, width), BF16)
    wide = jax.ShapeDtypeStruct((rows, width + EXTRA), BF16)
    row = jax.ShapeDtypeStruct((1, rows), F32)
    term = jax.ShapeDtypeStruct((rows, rows // 2), F32)
    terms = jax.ShapeDtypeStruct((2, rows, rows // 2), F32)
    total = jax.ShapeDtypeStruct((rows, width), F32)
    totals = jax.ShapeDtypeStruct((2, rows, width), F32)
    scratch = (pltpu.VMEM((rows, width), F32), pltpu.SemaphoreType.DMA((PIECES,)))

    even = lax.axis_index("grp") % 2 == 0
    x1 = move(jnp.where(even, texts, images), first_x)
    y1 = move(jnp.where(even, images, texts), first_y)
    (both,) = call(prepare_kernel, (double,), 1, (flags, images, texts))
    (pair1,) = call(stack_kernel, (double,), 0, (x1, y1))
    pair2 = move(pair1, later)
    mine = move(both, swap)
    pair3 = move(pair2, later)
    other = move(mine, cores)

    acc, above, small = call(
        early_kernel, (totals, terms, terms), 1, (scalars, mine, other, pair1, pair2)
    )
    pair3 = tied(pair3, acc)
    last = move(pair3[:LAST], later)
    (send_first,) = call(
        third_first_kernel, (wide,), 1, (scalars, other, pair3, acc, above, small)
    )
    back_first = move(send_first, home_first)
    acc, above, small = call(
        third_second_kernel,
        (total, term, term),
        1,
        (scalars, mine, tied(pair3, send_first), acc, above, small),
    )
    (send_second,) = call(
        fourth_kernel, (wide,), 1, (scalars, mine, tied(last, back_first), acc, above, small)
    )
    back_second = move(send_second, home_second)
    grad_images, grad_texts, loss = call(
        finish_first_kernel,
        (total, total, row),
        1,
        (flags, images, texts, tied(back_first, send_second)),
        outs_hbm=2,
        scratch=scratch,
    )
    grad_images, grad_texts, loss = call(
        finish_second_kernel,
        (total, total, row),
        1,
        (flags, images, texts, tied(back_second, loss), loss, grad_images, grad_texts),
        in_hbm=2,
        outs_hbm=2,
        scratch=scratch,
        aliases={5: 0, 6: 1},
    )
    return loss.reshape(rows), grad_images, grad_texts


def solution(mesh):
    return jax.shard_map(
        on_device,
        mesh=mesh,
        in_specs=(P(AXES, None), P(AXES, None), P(), P()),
        out_specs=(P(AXES), P(AXES, None), P(AXES, None)),
        check_vma=False,
    )
```

time: 253 us -> 127 us (0.50); the launches traced: 249 us -> 126 us
  waiting for transfers between devices: 193 us -> 32.6 us
  starting transfers between devices: 34.7 us -> 71.2 us
  Pallas kernels: 0 us -> 18.6 us
  matrix products: 11.6 us -> 0 us
  other arithmetic: 6.88 us -> 1.6 us
    ppermute x15 -> x9, waiting for transfers between devices: 193 us -> 32.6 us  [on_device(): move = lambda block, route: lax.ppermute(block, AXES, route)]
    ppermute x15 -> x9, starting transfers between devices: 34.7 us -> 71.2 us  [on_device(): move = lambda block, route: lax.ppermute(block, AXES, route)]
    pallas_call x0 -> x8, Pallas kernels: none -> 18.6 us  [call(): pl.pallas_call(kernel, out_shape=outs, in_specs=smem(n_smem) + vmem(len(a...]
    dot_general x24 -> x0, matrix products: 11.6 us -> none  [the longest x8 4.69 us: pairwise_loss_terms(): lax.dot_general(image_block_rows, text_block_rows, (((1,), (1,)), ((), ()...]
    mul x2 -> x0, other arithmetic: 2.58 us -> none  [back_norm(): return inverse * (grad_unit - unit32 * along)]
  transfers between devices with their start and end apart: 15 -> 9, of which waited for: 15 -> 5; matrix products, arithmetic and copies ran while one was open for 6% -> 0% of each run, Pallas kernels for 0% -> 11%
where the time goes in v2:
time: 127 us; the launch traced here: 126 us
  starting transfers between devices  71.2 us (56%)
  waiting for transfers between devices  32.6 us (26%)
  Pallas kernels  18.6 us (15%)
  between operations  2.12 us (2%)
  other arithmetic  1.6 us (1%)
    ppermute x9, starting transfers between devices, on_device(): move = lambda block, route: lax.ppermute(block, AXES, route)  71.2 us
    ppermute x9, waiting for transfers between devices, on_device(): move = lambda block, route: lax.ppermute(block, AXES, route)  32.6 us
    pallas_call x8, Pallas kernels, call(): pl.pallas_call(kernel, out_shape=outs, in_specs=smem(n_smem) + vmem(len(a...  18.6 us
  transfers between devices with their start and end apart: 9, of which 5 were waited for; matrix products, arithmetic and copies ran while one was open for 0% of the time, Pallas kernels for 11%

profile of v2, /device:TPU:1, one launch (start us, length us, event | category | flops | bytes accessed | tf_op | source)
XLA Modules:
  0.0 126.2 jit_solution(2358815582734354489)
XLA Ops:
  0.7 0.0 copy-start
  0.7 0.0 copy-start.1
  0.7 1.4 %broadcast_select_fusion = (bf16[256,1152]{1,0:T(8,128)(2,1)S(1)}, bf16[256,1152]{1,0:T(8,128)(2,1)S(1)}) fusion(bf16[256,1152]{1,0:T(8,128)(2,1)} %images.5, bf16[256,1152]{1,0:T(8,128)(2,1)} %texts.5, pred[]{:T(512)S(6)} %eq.7), kind=kLoop, calls=%fused_computation | loop fusion | flops 589824 | bytes 2359297 | tf_op jit(solution)/shard_map/jit(_where)/select_n | solution.py:284
  2.1 6.4 %collective-permute-start.1 = (bf16[256,1152]{1,0:T(8,128)(2,1)S(1)}, bf16[256,1152]{1,0:T(8,128)(2,1)S(1)}, u32[]{:S(2)}, u32[]{:S(2)}) collective-permute-start(bf16[256,1152]{1,0:T(8,128)(2,1)S(1)} %get-tuple-element.38), channel_id=1, source_target_pairs={{0,2},{2,4},{4,6},{6,8},{8,10},{10,13},{12,15},{14,17},{16,19},{18... | collective-permute-start | bytes 1769480 | tf_op jit(solution)/shard_map/ppermute | solution.py:271
  8.5 11.8 %collective-permute-start.2 = (bf16[256,1152]{1,0:T(8,128)(2,1)S(1)}, bf16[256,1152]{1,0:T(8,128)(2,1)S(1)}, u32[]{:S(2)}, u32[]{:S(2)}) collective-permute-start(bf16[256,1152]{1,0:T(8,128)(2,1)S(1)} %get-tuple-element.37), channel_id=1, source_target_pairs={{0,767},{2,24},{4,26},{6,28},{8,30},{10,32},{12,34},{14,37},{16,39... | collective-permute-start | bytes 1769480 | tf_op jit(solution)/shard_map/ppermute | solution.py:271
  20.4 0.1 pad_add_fusion.flags
  20.4 0.0 copy-done
  20.4 0.0 copy-done.1
  20.5 1.1 shard_map.67
  21.5 7.3 %collective-permute-start = (bf16[512,1152]{1,0:T(8,128)(2,1)S(1)}, bf16[512,1152]{1,0:T(8,128)(2,1)S(1)}, u32[]{:S(2)}, u32[]{:S(2)}) collective-permute-start(bf16[512,1152]{1,0:T(8,128)(2,1)S(1)} %shard_map.67), channel_id=1, source_target_pairs={{0,0},{1,24},{2,2},{3,26},{4,4},{5,28},{6,6},{7,30},{8,8},{9,32},{... | collective-permute-start | bytes 3538952 | tf_op jit(solution)/shard_map/ppermute | solution.py:271
  28.8 0.0 collective-permute-done.1.second
  28.8 1.5 %collective-permute-done.2.first = bf16[256,1152]{1,0:T(8,128)(2,1)S(1)} collective-permute-done((bf16[256,1152]{1,0:T(8,128)(2,1)S(1)}, bf16[256,1152]{1,0:T(8,128)(2,1)S(1)}, u32[]{:S(2)}, u32[]{:S(2)}) %collective-permute-start.2) | collective-permute-done | bytes 589856 | tf_op jit(solution)/shard_map/ppermute | solution.py:271
  30.3 0.4 shard_map.68.pair1
  30.7 16.7 %collective-permute-start.3 = (bf16[512,1152]{1,0:T(8,128)(2,1)S(1)}, bf16[512,1152]{1,0:T(8,128)(2,1)S(1)}, u32[]{:S(2)}, u32[]{:S(2)}) collective-permute-start(bf16[512,1152]{1,0:T(8,128)(2,1)S(1)} %shard_map.68.pair1), channel_id=1, source_target_pairs={{0,2},{2,4},{4,6},{6,8},{8,10},{10,13},{13,15},{15,17},{17,19},{19... | collective-permute-start | bytes 3538952 | tf_op jit(solution)/shard_map/ppermute | solution.py:271
  47.4 0.0 collective-permute-done.mine
  47.4 1.9 %collective-permute-start.5 = (bf16[512,1152]{1,0:T(8,128)(2,1)S(1)}, bf16[512,1152]{1,0:T(8,128)(2,1)S(1)}, u32[]{:S(2)}, u32[]{:S(2)}) collective-permute-start(bf16[512,1152]{1,0:T(8,128)(2,1)S(1)} %collective-permute-done.mine), channel_id=1, source_target_pairs={{0,24},{24,0},{2,26},{26,2},{4,28},{28,4},{6,30},{30,6},{8,32},{32... | collective-permute-start | bytes 3538952 | tf_op jit(solution)/shard_map/ppermute | solution.py:271
  49.3 11.2 %collective-permute-done.3.pair2 = bf16[512,1152]{1,0:T(8,128)(2,1)S(1)} collective-permute-done((bf16[512,1152]{1,0:T(8,128)(2,1)S(1)}, bf16[512,1152]{1,0:T(8,128)(2,1)S(1)}, u32[]{:S(2)}, u32[]{:S(2)}) %collective-permute-start.3) | collective-permute-done | bytes 1179680 | tf_op jit(solution)/shard_map/ppermute | solution.py:271
  60.5 14.0 %collective-permute-start.4 = (bf16[512,1152]{1,0:T(8,128)(2,1)S(1)}, bf16[512,1152]{1,0:T(8,128)(2,1)S(1)}, u32[]{:S(2)}, u32[]{:S(2)}) collective-permute-start(bf16[512,1152]{1,0:T(8,128)(2,1)S(1)} %collective-permute-done.3.pair2), channel_id=1, source_target_pairs={{0,2},{2,4},{4,6},{6,8},{8,10},{10,13},{13,15},{15,17},{17,19},{19... | collective-permute-start | bytes 3538952 | tf_op jit(solution)/shard_map/ppermute | solution.py:271
  75.8 0.1 pad_maximum_fusion.scalars
  75.9 0.0 collective-permute-done.5.other
  75.9 7.4 %shard_map.69 = (f32[2,256,1152]{2,1,0:T(8,128)S(1)}, f32[2,256,128]{2,1,0:T(8,128)S(1)}, f32[2,256,128]{2,1,0:T(8,128)S(1)}) custom-call(f32[2]{0:T(128)S(1)} %pad_maximum_fusion.scalars, bf16[512,1152]{1,0:T(8,128)(2,1)S(1)} %collective-permute-done.mine, bf16[512,1152]{1,0:T(8,128)(2,1)S(1)} %collective-permute-done.5.other, ...), custom_call_target="tpu_custom_call" | custom-call | flops 1 | bytes 1 | tf_op jit(solution)/shard_map/pallas_call | solution.py:218
  83.3 4.3 %collective-permute-done.4.pair3 = bf16[512,1152]{1,0:T(8,128)(2,1)S(1)} collective-permute-done((bf16[512,1152]{1,0:T(8,128)(2,1)S(1)}, bf16[512,1152]{1,0:T(8,128)(2,1)S(1)}, u32[]{:S(2)}, u32[]{:S(2)}) %collective-permute-start.4) | collective-permute-done | bytes 1179680 | tf_op jit(solution)/shard_map/ppermute | solution.py:271
  87.6 0.1 slice.3
  87.7 9.2 %collective-permute-start.6 = (bf16[288,1152]{1,0:T(8,128)(2,1)S(1)}, bf16[288,1152]{1,0:T(8,128)(2,1)S(1)}, u32[]{:S(2)}, u32[]{:S(2)}) collective-permute-start(bf16[288,1152]{1,0:T(8,128)(2,1)S(1)} %slice.3), channel_id=1, source_target_pairs={{0,2},{2,4},{4,6},{6,8},{8,10},{10,13},{13,15},{15,17},{17,19},{19... | collective-permute-start | bytes 1990664 | tf_op jit(solution)/shard_map/ppermute | solution.py:271
  96.9 1.7 %shard_map.70 = bf16[256,1280]{1,0:T(8,128)(2,1)S(1)} custom-call(f32[2]{0:T(128)S(1)} %pad_maximum_fusion.scalars, bf16[512,1152]{1,0:T(8,128)(2,1)S(1)} %collective-permute-done.5.other, bf16[512,1152]{1,0:T(8,128)(2,1)S(1)} %collective-permute-done.4.pair3, f32[2,256,1152]{2,1,0:T(8,128)S(1)} %get-tuple-element.20.acc, ...), custom_call_target="tpu_custom_call" | custom-call | flops 1 | bytes 1 | tf_op jit(solution)/shard_map/pallas_call | solution.py:218
  98.7 1.9 %collective-permute-start.7 = (bf16[256,1280]{1,0:T(8,128)(2,1)S(1)}, bf16[256,1280]{1,0:T(8,128)(2,1)S(1)}, u32[]{:S(2)}, u32[]{:S(2)}) collective-permute-start(bf16[256,1280]{1,0:T(8,128)(2,1)S(1)} %shard_map.70), channel_id=1, source_target_pairs={{0,1},{2,3},{4,5},{6,7},{8,9},{10,11},{13,13},{15,15},{17,17},{19,... | collective-permute-start | bytes 1966088 | tf_op jit(solution)/shard_map/ppermute | solution.py:271
  100.6 1.7 %shard_map.71 = (f32[256,1152]{1,0:T(8,128)S(1)}, f32[256,128]{1,0:T(8,128)S(1)}, f32[256,128]{1,0:T(8,128)S(1)}) custom-call(f32[2]{0:T(128)S(1)} %pad_maximum_fusion.scalars, bf16[512,1152]{1,0:T(8,128)(2,1)S(1)} %collective-permute-done.mine, bf16[512,1152]{1,0:T(8,128)(2,1)S(1)} %collective-permute-done.4.pair3, ...), custom_call_target="tpu_custom_call" | custom-call | flops 1 | bytes 1 | tf_op jit(solution)/shard_map/pallas_call | solution.py:218
  102.3 7.7 %collective-permute-done.7.block = bf16[256,1280]{1,0:T(8,128)(2,1)S(1)} collective-permute-done((bf16[256,1280]{1,0:T(8,128)(2,1)S(1)}, bf16[256,1280]{1,0:T(8,128)(2,1)S(1)}, u32[]{:S(2)}, u32[]{:S(2)}) %collective-permute-start.7) | collective-permute-done | bytes 655392 | tf_op jit(solution)/shard_map/ppermute | solution.py:271
  110.0 0.0 collective-permute-done.6.last
  110.0 1.6 %shard_map.72 = bf16[256,1280]{1,0:T(8,128)(2,1)S(1)} custom-call(f32[2]{0:T(128)S(1)} %pad_maximum_fusion.scalars, bf16[512,1152]{1,0:T(8,128)(2,1)S(1)} %collective-permute-done.mine, bf16[288,1152]{1,0:T(8,128)(2,1)S(1)} %collective-permute-done.6.last, f32[256,1152]{1,0:T(8,128)S(1)} %get-tuple-element.26.acc, f32[256,128]{1,0:T(8,128)S(1)} %get-tuple-element.27.above, ...), custom_call_target="tpu_custom_call" | custom-call | flops 1 | bytes 1 | tf_op jit(solution)/shard_map/pallas_call | solution.py:218
  111.6 1.9 %collective-permute-start.8 = (bf16[256,1280]{1,0:T(8,128)(2,1)S(1)}, bf16[256,1280]{1,0:T(8,128)(2,1)S(1)}, u32[]{:S(2)}, u32[]{:S(2)}) collective-permute-start(bf16[256,1280]{1,0:T(8,128)(2,1)S(1)} %shard_map.72), channel_id=1, source_target_pairs={{0,0},{2,2},{4,4},{6,6},{8,8},{10,10},{13,12},{15,14},{17,16},{19,... | collective-permute-start | bytes 1966088 | tf_op jit(solution)/shard_map/ppermute | solution.py:271
  113.5 2.1 %shard_map.73 = (f32[256,1152]{1,0:T(8,128)}, f32[256,1152]{1,0:T(8,128)}, f32[1,256]{1,0:T(1,128)S(1)}) custom-call(s32[2]{0:T(128)S(1)} %pad_add_fusion.flags, bf16[256,1152]{1,0:T(8,128)(2,1)S(1)} %copy-done, bf16[256,1152]{1,0:T(8,128)(2,1)S(1)} %copy-done.1, bf16[256,1280]{1,0:T(8,128)(2,1)S(1)} %collective-permute-done.7.block), custom_call_target="tpu_custom_call" | custom-call | flops 1 | bytes 1 | tf_op jit(solution)/shard_map/pallas_call | solution.py:218
  115.6 7.9 %collective-permute-done.8.block = bf16[256,1280]{1,0:T(8,128)(2,1)S(1)} collective-permute-done((bf16[256,1280]{1,0:T(8,128)(2,1)S(1)}, bf16[256,1280]{1,0:T(8,128)(2,1)S(1)}, u32[]{:S(2)}, u32[]{:S(2)}) %collective-permute-start.8) | collective-permute-done | bytes 655392 | tf_op jit(solution)/shard_map/ppermute | solution.py:271
  123.5 2.7 %shard_map.74 = (f32[256,1152]{1,0:T(8,128)}, f32[256,1152]{1,0:T(8,128)}, f32[1,256]{1,0:T(1,128)}) custom-call(s32[2]{0:T(128)S(1)} %pad_add_fusion.flags, bf16[256,1152]{1,0:T(8,128)(2,1)S(1)} %copy-done, bf16[256,1152]{1,0:T(8,128)(2,1)S(1)} %copy-done.1, ...), custom_call_target="tpu_custom_call", output_to_operand_aliasing={{0}: (5, {}), {1}: (6, {})} | custom-call | flops 1 | bytes 1 | tf_op jit(solution)/shard_map/pallas_call | solution.py:218
Async XLA Ops:
  0.7 19.8 %copy-start = (bf16[256,1152]{1,0:T(8,128)(2,1)S(1)}, bf16[256,1152]{1,0:T(8,128)(2,1)}, u32[]{:S(2)}) copy-start(bf16[256,1152]{1,0:T(8,128)(2,1)} %images.5) | copy-start | bytes 1769476
  0.7 19.8 %copy-start.1 = (bf16[256,1152]{1,0:T(8,128)(2,1)S(1)}, bf16[256,1152]{1,0:T(8,128)(2,1)}, u32[]{:S(2)}) copy-start(bf16[256,1152]{1,0:T(8,128)(2,1)} %texts.5) | copy-start | bytes 1769476
  2.1 26.7 %collective-permute-start.1 = (bf16[256,1152]{1,0:T(8,128)(2,1)S(1)}, bf16[256,1152]{1,0:T(8,128)(2,1)S(1)}, u32[]{:S(2)}, u32[]{:S(2)}) collective-permute-start(bf16[256,1152]{1,0:T(8,128)(2,1)S(1)} %get-tuple-element.38), channel_id=1, source_target_pairs={{0,2},{2,4},{4,6},{6,8},{8,10},{10,13},{12,15},{14,17},{16,19},{18... | collective-permute-start | bytes 1769480 | tf_op jit(solution)/shard_map/ppermute | solution.py:271
  8.5 21.8 %collective-permute-start.2 = (bf16[256,1152]{1,0:T(8,128)(2,1)S(1)}, bf16[256,1152]{1,0:T(8,128)(2,1)S(1)}, u32[]{:S(2)}, u32[]{:S(2)}) collective-permute-start(bf16[256,1152]{1,0:T(8,128)(2,1)S(1)} %get-tuple-element.37), channel_id=1, source_target_pairs={{0,767},{2,24},{4,26},{6,28},{8,30},{10,32},{12,34},{14,37},{16,39... | collective-permute-start | bytes 1769480 | tf_op jit(solution)/shard_map/ppermute | solution.py:271
  21.5 25.9 %collective-permute-start = (bf16[512,1152]{1,0:T(8,128)(2,1)S(1)}, bf16[512,1152]{1,0:T(8,128)(2,1)S(1)}, u32[]{:S(2)}, u32[]{:S(2)}) collective-permute-start(bf16[512,1152]{1,0:T(8,128)(2,1)S(1)} %shard_map.67), channel_id=1, source_target_pairs={{0,0},{1,24},{2,2},{3,26},{4,4},{5,28},{6,6},{7,30},{8,8},{9,32},{... | collective-permute-start | bytes 3538952 | tf_op jit(solution)/shard_map/ppermute | solution.py:271
  30.7 29.8 %collective-permute-start.3 = (bf16[512,1152]{1,0:T(8,128)(2,1)S(1)}, bf16[512,1152]{1,0:T(8,128)(2,1)S(1)}, u32[]{:S(2)}, u32[]{:S(2)}) collective-permute-start(bf16[512,1152]{1,0:T(8,128)(2,1)S(1)} %shard_map.68.pair1), channel_id=1, source_target_pairs={{0,2},{2,4},{4,6},{6,8},{8,10},{10,13},{13,15},{15,17},{17,19},{19... | collective-permute-start | bytes 3538952 | tf_op jit(solution)/shard_map/ppermute | solution.py:271
  47.4 28.5 %collective-permute-start.5 = (bf16[512,1152]{1,0:T(8,128)(2,1)S(1)}, bf16[512,1152]{1,0:T(8,128)(2,1)S(1)}, u32[]{:S(2)}, u32[]{:S(2)}) collective-permute-start(bf16[512,1152]{1,0:T(8,128)(2,1)S(1)} %collective-permute-done.mine), channel_id=1, source_target_pairs={{0,24},{24,0},{2,26},{26,2},{4,28},{28,4},{6,30},{30,6},{8,32},{32... | collective-permute-start | bytes 3538952 | tf_op jit(solution)/shard_map/ppermute | solution.py:271
  60.5 27.1 %collective-permute-start.4 = (bf16[512,1152]{1,0:T(8,128)(2,1)S(1)}, bf16[512,1152]{1,0:T(8,128)(2,1)S(1)}, u32[]{:S(2)}, u32[]{:S(2)}) collective-permute-start(bf16[512,1152]{1,0:T(8,128)(2,1)S(1)} %collective-permute-done.3.pair2), channel_id=1, source_target_pairs={{0,2},{2,4},{4,6},{6,8},{8,10},{10,13},{13,15},{15,17},{17,19},{19... | collective-permute-start | bytes 3538952 | tf_op jit(solution)/shard_map/ppermute | solution.py:271
  87.7 22.3 %collective-permute-start.6 = (bf16[288,1152]{1,0:T(8,128)(2,1)S(1)}, bf16[288,1152]{1,0:T(8,128)(2,1)S(1)}, u32[]{:S(2)}, u32[]{:S(2)}) collective-permute-start(bf16[288,1152]{1,0:T(8,128)(2,1)S(1)} %slice.3), channel_id=1, source_target_pairs={{0,2},{2,4},{4,6},{6,8},{8,10},{10,13},{13,15},{15,17},{17,19},{19... | collective-permute-start | bytes 1990664 | tf_op jit(solution)/shard_map/ppermute | solution.py:271
  98.7 11.3 %collective-permute-start.7 = (bf16[256,1280]{1,0:T(8,128)(2,1)S(1)}, bf16[256,1280]{1,0:T(8,128)(2,1)S(1)}, u32[]{:S(2)}, u32[]{:S(2)}) collective-permute-start(bf16[256,1280]{1,0:T(8,128)(2,1)S(1)} %shard_map.70), channel_id=1, source_target_pairs={{0,1},{2,3},{4,5},{6,7},{8,9},{10,11},{13,13},{15,15},{17,17},{19,... | collective-permute-start | bytes 1966088 | tf_op jit(solution)/shard_map/ppermute | solution.py:271
  111.6 11.9 %collective-permute-start.8 = (bf16[256,1280]{1,0:T(8,128)(2,1)S(1)}, bf16[256,1280]{1,0:T(8,128)(2,1)S(1)}, u32[]{:S(2)}, u32[]{:S(2)}) collective-permute-start(bf16[256,1280]{1,0:T(8,128)(2,1)S(1)} %shard_map.72), channel_id=1, source_target_pairs={{0,0},{2,2},{4,4},{6,6},{8,8},{10,10},{13,12},{15,14},{17,16},{19,... | collective-permute-start | bytes 1966088 | tf_op jit(solution)/shard_map/ppermute | solution.py:271

commit v3 on v2

--- a/solution.py
+++ b/solution.py
@@ -12,7 +12,7 @@
 F32 = jnp.float32
 EXTRA = 128
 PIECES = 4
-LAST = 288
+SPARE = 32
 
 
 def vmem(count):
@@ -29,27 +29,19 @@
     return wide * inverse, inverse
 
 
-def prepare_kernel(flags, images, texts, both):
+def prepare_kernel(flags, images, texts, x, y, both):
     rows = images.shape[0]
     img = unit_and_inverse(images[...])[0].astype(BF16)
     txt = unit_and_inverse(texts[...])[0].astype(BF16)
-    even = flags[1] == 0
-
-    @pl.when(even)
-    def _():
-        both[:rows] = txt
-        both[rows:] = img
-
-    @pl.when(jnp.logical_not(even))
-    def _():
-        both[:rows] = img
-        both[rows:] = txt
-
-
-def stack_kernel(second, first, stacked):
-    rows = first.shape[0]
-    stacked[:rows] = unit_and_inverse(first[...])[0].astype(BF16)
-    stacked[rows:] = unit_and_inverse(second[...])[0].astype(BF16)
+
+    def write(first, second):
+        x[...] = first
+        both[:rows] = first
+        y[...] = second
+        both[rows:] = second
+
+    pl.when(flags[1] == 0)(lambda: write(txt, img))
+    pl.when(flags[1] == 1)(lambda: write(img, txt))
 
 
 def joined(a, b):
@@ -95,14 +87,19 @@
     return total, total_above, total_small
 
 
-def early_kernel(scalars, mine, other, pair1, pair2, acc, above, small):
-    rows = mine.shape[0] // 2
-    later = [(c.at[at : at + rows], False) for c in (pair1, pair2) for at in (0, rows)]
-    first, second = (other.at[rows:], True), (mine.at[:rows], True)
+def whole(halves):
+    return jnp.concatenate([half[...] for half in halves], axis=0)
+
+
+def early_kernel(scalars, mine, low, middle, a1, b1, a2, b2, acc, above, small):
+    rows = a1.shape[0]
+    other = whole((low, middle))
+    other_x, other_y = other[:rows], other[rows:]
+    later = [(block, False) for block in (a1, b1, a2, b2)]
     acc[0], above[0], small[0] = side(
-        scalars, other[:rows], [first, (mine.at[:rows], False)] + later
-    )
-    acc[1], above[1], small[1] = side(scalars, mine[rows:], [second] + later)
+        scalars, other_x, [(other_y, True), (mine.at[:rows], False)] + later
+    )
+    acc[1], above[1], small[1] = side(scalars, mine[rows:], [(mine.at[:rows], True)] + later)
 
 
 def with_loss(out, grad, loss):
@@ -123,27 +120,22 @@
     return high + low
 
 
-def third_first_kernel(scalars, other, pair3, acc, above, small, send):
-    rows = other.shape[0] // 2
-    grad, more_above, more_small = side(
-        scalars, other[:rows], [(pair3.at[:rows], False), (pair3.at[rows:], False)]
-    )
+def third_first_kernel(scalars, low, middle, a3, b3, acc, above, small, send):
+    grad, more_above, more_small = side(scalars, whole((low, middle))[: a3.shape[0]], [(a3, False), (b3, False)])
     with_loss(send, acc[0] + grad, loss_of(above[0] + more_above, joined(small[0], more_small)))
 
 
-def third_second_kernel(scalars, mine, pair3, acc, above, small, new_acc, new_above, new_small):
-    rows = mine.shape[0] // 2
-    grad, more_above, more_small = side(
-        scalars, mine[rows:], [(pair3.at[:rows], False), (pair3.at[rows:], False)]
-    )
+def third_second_kernel(scalars, mine, a3, b3, acc, above, small, new_acc, new_above, new_small):
+    rows = a3.shape[0]
+    grad, more_above, more_small = side(scalars, mine[rows:], [(a3, False), (b3, False)])
     new_acc[...] = acc[1] + grad
     new_above[...] = above[1] + more_above
     new_small[...] = joined(small[1], more_small)
 
 
-def fourth_kernel(scalars, mine, last, acc, above, small, send):
+def fourth_kernel(scalars, mine, a4, acc, above, small, send):
     rows = mine.shape[0] // 2
-    grad, more_above, more_small = side(scalars, mine[rows:], [(last.at[:rows], False)])
+    grad, more_above, more_small = side(scalars, mine[rows:], [(a4.at[:rows], False)])
     with_loss(
         send, acc[...] + grad, loss_of(above[...] + more_above, joined(small[...], more_small))
     )
@@ -279,34 +271,34 @@
     totals = jax.ShapeDtypeStruct((2, rows, width), F32)
     scratch = (pltpu.VMEM((rows, width), F32), pltpu.SemaphoreType.DMA((PIECES,)))
 
-    even = lax.axis_index("grp") % 2 == 0
-    x1 = move(jnp.where(even, texts, images), first_x)
-    y1 = move(jnp.where(even, images, texts), first_y)
-    (both,) = call(prepare_kernel, (double,), 1, (flags, images, texts))
-    (pair1,) = call(stack_kernel, (double,), 0, (x1, y1))
-    pair2 = move(pair1, later)
+    block = jax.ShapeDtypeStruct((rows, width), BF16)
+    x, y, both = call(prepare_kernel, (block, block, double), 1, (flags, images, texts))
+    b1, a1 = move(x, first_x), move(y, first_y)
+    b2, a2 = move(b1, later), move(a1, later)
+    b3, a3 = move(b2, later), move(a2, later)
     mine = move(both, swap)
-    pair3 = move(pair2, later)
-    other = move(mine, cores)
+    step = rows
+    other = [move(mine[at : at + step], cores) for at in range(0, 2 * rows, step)]
 
     acc, above, small = call(
-        early_kernel, (totals, terms, terms), 1, (scalars, mine, other, pair1, pair2)
-    )
-    pair3 = tied(pair3, acc)
-    last = move(pair3[:LAST], later)
+        early_kernel,
+        (totals, terms, terms),
+        1,
+        (scalars, tied(mine, a3), *other, a1, b1, a2, b2),
+    )
+    a4 = move(jnp.concatenate([a3, a2[:SPARE]]), later)
     (send_first,) = call(
-        third_first_kernel, (wide,), 1, (scalars, other, pair3, acc, above, small)
+        third_first_kernel, (wide,), 1, (scalars, *other[:2], a3, b3, acc, above, small)
     )
     back_first = move(send_first, home_first)
     acc, above, small = call(
         third_second_kernel,
         (total, term, term),
         1,
-        (scalars, mine, tied(pair3, send_first), acc, above, small),
-    )
-    (send_second,) = call(
-        fourth_kernel, (wide,), 1, (scalars, mine, tied(last, back_first), acc, above, small)
-    )
+        (scalars, mine, tied(a3, send_first), b3, acc, above, small),
+    )
+    (send_second,) = call(fourth_kernel, (wide,), 1, (scalars, mine, a4, acc, above, small))
+    send_second = tied(send_second, back_first)
     back_second = move(send_second, home_second)
     grad_images, grad_texts, loss = call(
         finish_first_kernel,

time: 127 us -> 124 us (0.976)
  waiting for transfers between devices: 32.6 us -> 21.4 us
  starting transfers between devices: 71.2 us -> 79.2 us
  local copies, waits for them, and re-layouts: 0.06 us -> 2.24 us
  other arithmetic: 1.6 us -> 0.21 us
    ppermute x9 -> x12, waiting for transfers between devices: 32.6 us -> 21.4 us  [on_device(): move = lambda block, route: lax.ppermute(block, AXES, route)]
    ppermute x9 -> x12, starting transfers between devices: 71.2 us -> 79.2 us  [on_device(): move = lambda block, route: lax.ppermute(block, AXES, route)]
    unnamed x4 -> x8, local copies, waits for them, and re-layouts: 0.01 us -> 2.14 us
    select_n x1 -> x0, other arithmetic: 1.45 us -> none  [on_device(): y1 = move(jnp.where(even, images, texts), first_y)]
    pallas_call x8 -> x7, Pallas kernels: 18.6 us -> 18.3 us  [call(): pl.pallas_call(kernel, out_shape=outs, in_specs=smem(n_smem) + vmem(len(a...]
  transfers between devices with their start and end apart: 9 -> 12, of which waited for: 5 -> 4; matrix products, arithmetic and copies ran while one was open for 0% -> 0% of each run, Pallas kernels for 11% -> 12%
where the time goes in v3:
time: 124 us
  starting transfers between devices  79.2 us (64%)
  waiting for transfers between devices  21.4 us (17%)
  Pallas kernels  18.3 us (15%)
  local copies, waits for them, and re-layouts  2.24 us (2%)
  between operations  2.2 us (2%)
    ppermute x12, starting transfers between devices, on_device(): move = lambda block, route: lax.ppermute(block, AXES, route)  79.2 us
    ppermute x12, waiting for transfers between devices, on_device(): move = lambda block, route: lax.ppermute(block, AXES, route)  21.4 us
    pallas_call x7, Pallas kernels, call(): pl.pallas_call(kernel, out_shape=outs, in_specs=smem(n_smem) + vmem(len(a...  18.3 us
  transfers between devices with their start and end apart: 12, of which 4 were waited for; matrix products, arithmetic and copies ran while one was open for 0% of the time, Pallas kernels for 12%

profile of v3, /device:TPU:1, one launch (start us, length us, event | category | flops | bytes accessed | tf_op | source)
XLA Modules:
  0.0 123.5 jit_solution(196019134107763442)
XLA Ops:
  0.7 0.1 pad_add_fusion.flags
  0.7 0.0 copy-start
  0.7 1.1 copy-done
  1.8 0.0 copy-start.2
  1.8 1.1 copy-done.2
  2.9 1.1 shard_map.67
  4.0 16.1 %collective-permute-start.1 = (bf16[256,1152]{1,0:T(8,128)(2,1)S(1)}, bf16[256,1152]{1,0:T(8,128)(2,1)S(1)}, u32[]{:S(2)}, u32[]{:S(2)}) collective-permute-start(bf16[256,1152]{1,0:T(8,128)(2,1)S(1)} %get-tuple-element.24), channel_id=1, source_target_pairs={{0,767},{2,24},{4,26},{6,28},{8,30},{10,32},{12,34},{14,37},{16,39... | collective-permute-start | bytes 1769480 | tf_op jit(solution)/shard_map/ppermute | solution.py:263
  20.1 1.9 %collective-permute-start = (bf16[512,1152]{1,0:T(8,128)(2,1)S(1)}, bf16[512,1152]{1,0:T(8,128)(2,1)S(1)}, u32[]{:S(2)}, u32[]{:S(2)}) collective-permute-start(bf16[512,1152]{1,0:T(8,128)(2,1)S(1)} %get-tuple-element.23), channel_id=1, source_target_pairs={{0,0},{1,24},{2,2},{3,26},{4,4},{5,28},{6,6},{7,30},{8,8},{9,32},{... | collective-permute-start | bytes 3538952 | tf_op jit(solution)/shard_map/ppermute | solution.py:263
  22.1 1.9 %collective-permute-start.7 = (bf16[256,1152]{1,0:T(8,128)(2,1)S(1)}, bf16[256,1152]{1,0:T(8,128)(2,1)S(1)}, u32[]{:S(2)}, u32[]{:S(2)}) collective-permute-start(bf16[256,1152]{1,0:T(8,128)(2,1)S(1)} %get-tuple-element.25), channel_id=1, source_target_pairs={{0,2},{2,4},{4,6},{6,8},{8,10},{10,13},{12,15},{14,17},{16,19},{18... | collective-permute-start | bytes 1769480 | tf_op jit(solution)/shard_map/ppermute | solution.py:263
  24.0 4.6 %collective-permute-done.1.a1 = bf16[256,1152]{1,0:T(8,128)(2,1)S(1)} collective-permute-done((bf16[256,1152]{1,0:T(8,128)(2,1)S(1)}, bf16[256,1152]{1,0:T(8,128)(2,1)S(1)}, u32[]{:S(2)}, u32[]{:S(2)}) %collective-permute-start.1) | collective-permute-done | bytes 589856 | tf_op jit(solution)/shard_map/ppermute | solution.py:263
  28.6 16.6 %collective-permute-start.2 = (bf16[256,1152]{1,0:T(8,128)(2,1)S(1)}, bf16[256,1152]{1,0:T(8,128)(2,1)S(1)}, u32[]{:S(2)}, u32[]{:S(2)}) collective-permute-start(bf16[256,1152]{1,0:T(8,128)(2,1)S(1)} %collective-permute-done.1.a1), channel_id=1, source_target_pairs={{0,2},{2,4},{4,6},{6,8},{8,10},{10,13},{13,15},{15,17},{17,19},{19... | collective-permute-start | bytes 1769480 | tf_op jit(solution)/shard_map/ppermute | solution.py:263
  45.3 0.0 collective-permute-done.7.b1
  45.3 4.0 %collective-permute-start.8 = (bf16[256,1152]{1,0:T(8,128)(2,1)S(1)}, bf16[256,1152]{1,0:T(8,128)(2,1)S(1)}, u32[]{:S(2)}, u32[]{:S(2)}) collective-permute-start(bf16[256,1152]{1,0:T(8,128)(2,1)S(1)} %collective-permute-done.7.b1), channel_id=1, source_target_pairs={{0,2},{2,4},{4,6},{6,8},{8,10},{10,13},{13,15},{15,17},{17,19},{19... | collective-permute-start | bytes 1769480 | tf_op jit(solution)/shard_map/ppermute | solution.py:263
  49.2 2.8 %collective-permute-done.2.a2 = bf16[256,1152]{1,0:T(8,128)(2,1)S(1)} collective-permute-done((bf16[256,1152]{1,0:T(8,128)(2,1)S(1)}, bf16[256,1152]{1,0:T(8,128)(2,1)S(1)}, u32[]{:S(2)}, u32[]{:S(2)}) %collective-permute-start.2) | collective-permute-done | bytes 589856 | tf_op jit(solution)/shard_map/ppermute | solution.py:263
  52.1 9.2 %collective-permute-start.3 = (bf16[256,1152]{1,0:T(8,128)(2,1)S(1)}, bf16[256,1152]{1,0:T(8,128)(2,1)S(1)}, u32[]{:S(2)}, u32[]{:S(2)}) collective-permute-start(bf16[256,1152]{1,0:T(8,128)(2,1)S(1)} %collective-permute-done.2.a2), channel_id=1, source_target_pairs={{0,2},{2,4},{4,6},{6,8},{8,10},{10,13},{13,15},{15,17},{17,19},{19... | collective-permute-start | bytes 1769480 | tf_op jit(solution)/shard_map/ppermute | solution.py:263
  61.3 0.0 collective-permute-done.mine
  61.3 0.1 fusion
  61.4 1.9 %collective-permute-start.5 = (bf16[256,1152]{1,0:T(8,128)(2,1)S(1)}, bf16[256,1152]{1,0:T(8,128)(2,1)S(1)}, u32[]{:S(2)}, u32[]{:S(2)}) collective-permute-start(bf16[256,1152]{1,0:T(8,128)(2,1)S(1)} %get-tuple-element.44), channel_id=1, source_target_pairs={{0,24},{24,0},{2,26},{26,2},{4,28},{28,4},{6,30},{30,6},{8,32},{32... | collective-permute-start | bytes 1769480 | tf_op jit(solution)/shard_map/ppermute | solution.py:263
  63.4 2.4 %collective-permute-start.6 = (bf16[256,1152]{1,0:T(8,128)(2,1)S(1)}, bf16[256,1152]{1,0:T(8,128)(2,1)S(1)}, u32[]{:S(2)}, u32[]{:S(2)}) collective-permute-start(bf16[256,1152]{1,0:T(8,128)(2,1)S(1)} %get-tuple-element.43), channel_id=1, source_target_pairs={{0,24},{24,0},{2,26},{26,2},{4,28},{28,4},{6,30},{30,6},{8,32},{32... | collective-permute-start | bytes 1769480 | tf_op jit(solution)/shard_map/ppermute | solution.py:263
  65.8 0.0 collective-permute-done.8.b2
  65.8 19.3 %collective-permute-start.9 = (bf16[256,1152]{1,0:T(8,128)(2,1)S(1)}, bf16[256,1152]{1,0:T(8,128)(2,1)S(1)}, u32[]{:S(2)}, u32[]{:S(2)}) collective-permute-start(bf16[256,1152]{1,0:T(8,128)(2,1)S(1)} %collective-permute-done.8.b2), channel_id=1, source_target_pairs={{0,2},{2,4},{4,6},{6,8},{8,10},{10,13},{13,15},{15,17},{17,19},{19... | collective-permute-start | bytes 1769480 | tf_op jit(solution)/shard_map/ppermute | solution.py:263
  86.4 0.0 collective-permute-done.3.a3
  86.4 0.1 pad_maximum_fusion
  86.5 1.9 %collective-permute-start.4 = (bf16[288,1152]{1,0:T(8,128)(2,1)S(1)}, bf16[288,1152]{1,0:T(8,128)(2,1)S(1)}, u32[]{:S(2)}, u32[]{:S(2)}) collective-permute-start(bf16[288,1152]{1,0:T(8,128)(2,1)S(1)} %pad_maximum_fusion), channel_id=1, source_target_pairs={{0,2},{2,4},{4,6},{6,8},{8,10},{10,13},{13,15},{15,17},{17,19},{19... | collective-permute-start | bytes 1990664 | tf_op jit(solution)/shard_map/ppermute | solution.py:263
  88.4 0.1 pad_maximum_fusion.1.scalars
  88.5 0.0 collective-permute-done.5.low
  88.5 0.0 collective-permute-done.6.middle
  88.5 7.4 %shard_map.68 = (f32[2,256,1152]{2,1,0:T(8,128)S(1)}, f32[2,256,128]{2,1,0:T(8,128)S(1)}, f32[2,256,128]{2,1,0:T(8,128)S(1)}) custom-call(f32[2]{0:T(128)S(1)} %pad_maximum_fusion.1.scalars, bf16[512,1152]{1,0:T(8,128)(2,1)S(1)} %collective-permute-done.mine, bf16[256,1152]{1,0:T(8,128)(2,1)S(1)} %collective-permute-done.5.low, ...), custom_call_target="tpu_custom_call" | custom-call | flops 1 | bytes 1 | tf_op jit(solution)/shard_map/pallas_call | solution.py:210
  95.9 0.0 collective-permute-done.9.b3
  95.9 1.7 %shard_map.69 = bf16[256,1280]{1,0:T(8,128)(2,1)S(1)} custom-call(f32[2]{0:T(128)S(1)} %pad_maximum_fusion.1.scalars, bf16[256,1152]{1,0:T(8,128)(2,1)S(1)} %collective-permute-done.5.low, bf16[256,1152]{1,0:T(8,128)(2,1)S(1)} %collective-permute-done.6.middle, bf16[256,1152]{1,0:T(8,128)(2,1)S(1)} %collective-permute-done.3.a3, ...), custom_call_target="tpu_custom_call" | custom-call | flops 1 | bytes 1 | tf_op jit(solution)/shard_map/pallas_call | solution.py:210
  97.7 1.9 %collective-permute-start.10 = (bf16[256,1280]{1,0:T(8,128)(2,1)S(1)}, bf16[256,1280]{1,0:T(8,128)(2,1)S(1)}, u32[]{:S(2)}, u32[]{:S(2)}) collective-permute-start(bf16[256,1280]{1,0:T(8,128)(2,1)S(1)} %shard_map.69), channel_id=1, source_target_pairs={{0,1},{2,3},{4,5},{6,7},{8,9},{10,11},{13,13},{15,15},{17,17},{19,... | collective-permute-start | bytes 1966088 | tf_op jit(solution)/shard_map/ppermute | solution.py:263
  99.6 1.7 %shard_map.70 = (f32[256,1152]{1,0:T(8,128)S(1)}, f32[256,128]{1,0:T(8,128)S(1)}, f32[256,128]{1,0:T(8,128)S(1)}) custom-call(f32[2]{0:T(128)S(1)} %pad_maximum_fusion.1.scalars, bf16[512,1152]{1,0:T(8,128)(2,1)S(1)} %collective-permute-done.mine, bf16[256,1152]{1,0:T(8,128)(2,1)S(1)} %collective-permute-done.3.a3, ...), custom_call_target="tpu_custom_call" | custom-call | flops 1 | bytes 1 | tf_op jit(solution)/shard_map/pallas_call | solution.py:210
  101.3 0.0 collective-permute-done.4.a4
  101.3 0.0 copy-start.1
  101.3 0.0 copy-start.3
  101.4 1.6 %shard_map.71 = bf16[256,1280]{1,0:T(8,128)(2,1)S(1)} custom-call(f32[2]{0:T(128)S(1)} %pad_maximum_fusion.1.scalars, bf16[512,1152]{1,0:T(8,128)(2,1)S(1)} %collective-permute-done.mine, bf16[288,1152]{1,0:T(8,128)(2,1)S(1)} %collective-permute-done.4.a4, f32[256,1152]{1,0:T(8,128)S(1)} %get-tuple-element.31.acc, f32[256,128]{1,0:T(8,128)S(1)} %get-tuple-element.32.above, ...), custom_call_target="tpu_custom_call" | custom-call | flops 1 | bytes 1 | tf_op jit(solution)/shard_map/pallas_call | solution.py:210
  102.9 6.1 %collective-permute-done.10.block = bf16[256,1280]{1,0:T(8,128)(2,1)S(1)} collective-permute-done((bf16[256,1280]{1,0:T(8,128)(2,1)S(1)}, bf16[256,1280]{1,0:T(8,128)(2,1)S(1)}, u32[]{:S(2)}, u32[]{:S(2)}) %collective-permute-start.10) | collective-permute-done | bytes 655392 | tf_op jit(solution)/shard_map/ppermute | solution.py:263
  109.0 1.9 %collective-permute-start.11 = (bf16[256,1280]{1,0:T(8,128)(2,1)S(1)}, bf16[256,1280]{1,0:T(8,128)(2,1)S(1)}, u32[]{:S(2)}, u32[]{:S(2)}) collective-permute-start(bf16[256,1280]{1,0:T(8,128)(2,1)S(1)} %shard_map.71), channel_id=1, source_target_pairs={{0,0},{2,2},{4,4},{6,6},{8,8},{10,10},{13,12},{15,14},{17,16},{19,... | collective-permute-start | bytes 1966088 | tf_op jit(solution)/shard_map/ppermute | solution.py:263
  110.9 0.0 copy-done.1
  110.9 0.0 copy-done.3
  110.9 2.1 %shard_map.72 = (f32[256,1152]{1,0:T(8,128)}, f32[256,1152]{1,0:T(8,128)}, f32[1,256]{1,0:T(1,128)S(1)}) custom-call(s32[2]{0:T(128)S(1)} %pad_add_fusion.flags, bf16[256,1152]{1,0:T(8,128)(2,1)S(1)} %copy-done.1, bf16[256,1152]{1,0:T(8,128)(2,1)S(1)} %copy-done.3, bf16[256,1280]{1,0:T(8,128)(2,1)S(1)} %collective-permute-done.10.block), custom_call_target="tpu_custom_call" | custom-call | flops 1 | bytes 1 | tf_op jit(solution)/shard_map/pallas_call | solution.py:210
  113.0 7.9 %collective-permute-done.11.block = bf16[256,1280]{1,0:T(8,128)(2,1)S(1)} collective-permute-done((bf16[256,1280]{1,0:T(8,128)(2,1)S(1)}, bf16[256,1280]{1,0:T(8,128)(2,1)S(1)}, u32[]{:S(2)}, u32[]{:S(2)}) %collective-permute-start.11) | collective-permute-done | bytes 655392 | tf_op jit(solution)/shard_map/ppermute | solution.py:263
  120.9 2.7 %shard_map.73 = (f32[256,1152]{1,0:T(8,128)}, f32[256,1152]{1,0:T(8,128)}, f32[1,256]{1,0:T(1,128)}) custom-call(s32[2]{0:T(128)S(1)} %pad_add_fusion.flags, bf16[256,1152]{1,0:T(8,128)(2,1)S(1)} %copy-done.1, bf16[256,1152]{1,0:T(8,128)(2,1)S(1)} %copy-done.3, ...), custom_call_target="tpu_custom_call", output_to_operand_aliasing={{0}: (5, {}), {1}: (6, {})} | custom-call | flops 1 | bytes 1 | tf_op jit(solution)/shard_map/pallas_call | solution.py:210
  (1 shorter events, 0.0 us)
Async XLA Ops:
  0.7 1.1 copy-start
  1.8 1.1 copy-start.2
  4.0 24.6 %collective-permute-start.1 = (bf16[256,1152]{1,0:T(8,128)(2,1)S(1)}, bf16[256,1152]{1,0:T(8,128)(2,1)S(1)}, u32[]{:S(2)}, u32[]{:S(2)}) collective-permute-start(bf16[256,1152]{1,0:T(8,128)(2,1)S(1)} %get-tuple-element.24), channel_id=1, source_target_pairs={{0,767},{2,24},{4,26},{6,28},{8,30},{10,32},{12,34},{14,37},{16,39... | collective-permute-start | bytes 1769480 | tf_op jit(solution)/shard_map/ppermute | solution.py:263
  20.1 41.2 %collective-permute-start = (bf16[512,1152]{1,0:T(8,128)(2,1)S(1)}, bf16[512,1152]{1,0:T(8,128)(2,1)S(1)}, u32[]{:S(2)}, u32[]{:S(2)}) collective-permute-start(bf16[512,1152]{1,0:T(8,128)(2,1)S(1)} %get-tuple-element.23), channel_id=1, source_target_pairs={{0,0},{1,24},{2,2},{3,26},{4,4},{5,28},{6,6},{7,30},{8,8},{9,32},{... | collective-permute-start | bytes 3538952 | tf_op jit(solution)/shard_map/ppermute | solution.py:263
  22.1 23.2 %collective-permute-start.7 = (bf16[256,1152]{1,0:T(8,128)(2,1)S(1)}, bf16[256,1152]{1,0:T(8,128)(2,1)S(1)}, u32[]{:S(2)}, u32[]{:S(2)}) collective-permute-start(bf16[256,1152]{1,0:T(8,128)(2,1)S(1)} %get-tuple-element.25), channel_id=1, source_target_pairs={{0,2},{2,4},{4,6},{6,8},{8,10},{10,13},{12,15},{14,17},{16,19},{18... | collective-permute-start | bytes 1769480 | tf_op jit(solution)/shard_map/ppermute | solution.py:263
  28.6 23.5 %collective-permute-start.2 = (bf16[256,1152]{1,0:T(8,128)(2,1)S(1)}, bf16[256,1152]{1,0:T(8,128)(2,1)S(1)}, u32[]{:S(2)}, u32[]{:S(2)}) collective-permute-start(bf16[256,1152]{1,0:T(8,128)(2,1)S(1)} %collective-permute-done.1.a1), channel_id=1, source_target_pairs={{0,2},{2,4},{4,6},{6,8},{8,10},{10,13},{13,15},{15,17},{17,19},{19... | collective-permute-start | bytes 1769480 | tf_op jit(solution)/shard_map/ppermute | solution.py:263
  45.3 20.5 %collective-permute-start.8 = (bf16[256,1152]{1,0:T(8,128)(2,1)S(1)}, bf16[256,1152]{1,0:T(8,128)(2,1)S(1)}, u32[]{:S(2)}, u32[]{:S(2)}) collective-permute-start(bf16[256,1152]{1,0:T(8,128)(2,1)S(1)} %collective-permute-done.7.b1), channel_id=1, source_target_pairs={{0,2},{2,4},{4,6},{6,8},{8,10},{10,13},{13,15},{15,17},{17,19},{19... | collective-permute-start | bytes 1769480 | tf_op jit(solution)/shard_map/ppermute | solution.py:263
  52.1 34.3 %collective-permute-start.3 = (bf16[256,1152]{1,0:T(8,128)(2,1)S(1)}, bf16[256,1152]{1,0:T(8,128)(2,1)S(1)}, u32[]{:S(2)}, u32[]{:S(2)}) collective-permute-start(bf16[256,1152]{1,0:T(8,128)(2,1)S(1)} %collective-permute-done.2.a2), channel_id=1, source_target_pairs={{0,2},{2,4},{4,6},{6,8},{8,10},{10,13},{13,15},{15,17},{17,19},{19... | collective-permute-start | bytes 1769480 | tf_op jit(solution)/shard_map/ppermute | solution.py:263
  61.4 27.1 %collective-permute-start.5 = (bf16[256,1152]{1,0:T(8,128)(2,1)S(1)}, bf16[256,1152]{1,0:T(8,128)(2,1)S(1)}, u32[]{:S(2)}, u32[]{:S(2)}) collective-permute-start(bf16[256,1152]{1,0:T(8,128)(2,1)S(1)} %get-tuple-element.44), channel_id=1, source_target_pairs={{0,24},{24,0},{2,26},{26,2},{4,28},{28,4},{6,30},{30,6},{8,32},{32... | collective-permute-start | bytes 1769480 | tf_op jit(solution)/shard_map/ppermute | solution.py:263
  63.4 25.1 %collective-permute-start.6 = (bf16[256,1152]{1,0:T(8,128)(2,1)S(1)}, bf16[256,1152]{1,0:T(8,128)(2,1)S(1)}, u32[]{:S(2)}, u32[]{:S(2)}) collective-permute-start(bf16[256,1152]{1,0:T(8,128)(2,1)S(1)} %get-tuple-element.43), channel_id=1, source_target_pairs={{0,24},{24,0},{2,26},{26,2},{4,28},{28,4},{6,30},{30,6},{8,32},{32... | collective-permute-start | bytes 1769480 | tf_op jit(solution)/shard_map/ppermute | solution.py:263
  65.8 30.1 %collective-permute-start.9 = (bf16[256,1152]{1,0:T(8,128)(2,1)S(1)}, bf16[256,1152]{1,0:T(8,128)(2,1)S(1)}, u32[]{:S(2)}, u32[]{:S(2)}) collective-permute-start(bf16[256,1152]{1,0:T(8,128)(2,1)S(1)} %collective-permute-done.8.b2), channel_id=1, source_target_pairs={{0,2},{2,4},{4,6},{6,8},{8,10},{10,13},{13,15},{15,17},{17,19},{19... | collective-permute-start | bytes 1769480 | tf_op jit(solution)/shard_map/ppermute | solution.py:263
  86.5 14.9 %collective-permute-start.4 = (bf16[288,1152]{1,0:T(8,128)(2,1)S(1)}, bf16[288,1152]{1,0:T(8,128)(2,1)S(1)}, u32[]{:S(2)}, u32[]{:S(2)}) collective-permute-start(bf16[288,1152]{1,0:T(8,128)(2,1)S(1)} %pad_maximum_fusion), channel_id=1, source_target_pairs={{0,2},{2,4},{4,6},{6,8},{8,10},{10,13},{13,15},{15,17},{17,19},{19... | collective-permute-start | bytes 1990664 | tf_op jit(solution)/shard_map/ppermute | solution.py:263
  97.7 11.3 %collective-permute-start.10 = (bf16[256,1280]{1,0:T(8,128)(2,1)S(1)}, bf16[256,1280]{1,0:T(8,128)(2,1)S(1)}, u32[]{:S(2)}, u32[]{:S(2)}) collective-permute-start(bf16[256,1280]{1,0:T(8,128)(2,1)S(1)} %shard_map.69), channel_id=1, source_target_pairs={{0,1},{2,3},{4,5},{6,7},{8,9},{10,11},{13,13},{15,15},{17,17},{19,... | collective-permute-start | bytes 1966088 | tf_op jit(solution)/shard_map/ppermute | solution.py:263
  101.3 9.6 %copy-start.1 = (bf16[256,1152]{1,0:T(8,128)(2,1)S(1)}, bf16[256,1152]{1,0:T(8,128)(2,1)}, u32[]{:S(2)}) copy-start(bf16[256,1152]{1,0:T(8,128)(2,1)} %images.5) | copy-start | bytes 1769476
  101.3 9.6 %copy-start.3 = (bf16[256,1152]{1,0:T(8,128)(2,1)S(1)}, bf16[256,1152]{1,0:T(8,128)(2,1)}, u32[]{:S(2)}) copy-start(bf16[256,1152]{1,0:T(8,128)(2,1)} %texts.5) | copy-start | bytes 1769476
  109.0 11.9 %collective-permute-start.11 = (bf16[256,1280]{1,0:T(8,128)(2,1)S(1)}, bf16[256,1280]{1,0:T(8,128)(2,1)S(1)}, u32[]{:S(2)}, u32[]{:S(2)}) collective-permute-start(bf16[256,1280]{1,0:T(8,128)(2,1)S(1)} %shard_map.71), channel_id=1, source_target_pairs={{0,0},{2,2},{4,4},{6,6},{8,8},{10,10},{13,12},{15,14},{17,16},{19,... | collective-permute-start | bytes 1966088 | tf_op jit(solution)/shard_map/ppermute | solution.py:263

commit v4 on v3

--- a/solution.py
+++ b/solution.py
@@ -230,8 +230,9 @@
 
     def held_at(block):
         blk, grp = divmod(block, grps)
-        turns = blk // 2 % 4 != 3
-        column = (blk + (turns and grp >= grps // 2)) % 2
+        across = blk // 2 % 4
+        turns = across != 1
+        column = (blk + (across > 1) + (turns and grp >= grps // 2)) % 2
         return blk - blk % 2, grp - grp % 2 + column
 
     def on_core(block, core):

time: 124 us -> 119 us (0.960)
  the two profiles are of different devices: /device:TPU:1 before, /device:TPU:3 now
where the time goes in v4:
time: 119 us
  starting transfers between devices  52.5 us (44%)
  waiting for transfers between devices  43.3 us (36%)
  Pallas kernels  18.3 us (15%)
  local copies, waits for them, and re-layouts  2.24 us (2%)
  between operations  2.19 us (2%)
    ppermute x12, starting transfers between devices, on_device(): move = lambda block, route: lax.ppermute(block, AXES, route)  52.5 us
    ppermute x12, waiting for transfers between devices, on_device(): move = lambda block, route: lax.ppermute(block, AXES, route)  43.3 us
    pallas_call x7, Pallas kernels, call(): pl.pallas_call(kernel, out_shape=outs, in_specs=smem(n_smem) + vmem(len(a...  18.3 us
  transfers between devices with their start and end apart: 12, of which 4 were waited for; matrix products, arithmetic and copies ran while one was open for 0% of the time, Pallas kernels for 12%

profile of v4, /device:TPU:3, one launch (start us, length us, event | category | flops | bytes accessed | tf_op | source)
XLA Modules:
  0.0 118.7 jit_solution(2643228049617426192)
XLA Ops:
  0.7 0.1 pad_add_fusion.flags
  0.7 0.0 copy-start
  0.7 1.1 copy-done
  1.8 0.0 copy-start.2
  1.8 1.1 copy-done.2
  2.9 1.1 shard_map.67
  4.0 14.3 %collective-permute-start.1 = (bf16[256,1152]{1,0:T(8,128)(2,1)S(1)}, bf16[256,1152]{1,0:T(8,128)(2,1)S(1)}, u32[]{:S(2)}, u32[]{:S(2)}) collective-permute-start(bf16[256,1152]{1,0:T(8,128)(2,1)S(1)} %get-tuple-element.24), channel_id=1, source_target_pairs={{0,767},{2,24},{4,26},{6,28},{8,30},{10,32},{12,34},{14,37},{16,39... | collective-permute-start | bytes 1769480 | tf_op jit(solution)/shard_map/ppermute | solution.py:264
  18.3 1.9 %collective-permute-start = (bf16[512,1152]{1,0:T(8,128)(2,1)S(1)}, bf16[512,1152]{1,0:T(8,128)(2,1)S(1)}, u32[]{:S(2)}, u32[]{:S(2)}) collective-permute-start(bf16[512,1152]{1,0:T(8,128)(2,1)S(1)} %get-tuple-element.23), channel_id=1, source_target_pairs={{0,0},{1,24},{2,2},{3,26},{4,4},{5,28},{6,6},{7,30},{8,8},{9,32},{... | collective-permute-start | bytes 3538952 | tf_op jit(solution)/shard_map/ppermute | solution.py:264
  20.2 1.9 %collective-permute-start.7 = (bf16[256,1152]{1,0:T(8,128)(2,1)S(1)}, bf16[256,1152]{1,0:T(8,128)(2,1)S(1)}, u32[]{:S(2)}, u32[]{:S(2)}) collective-permute-start(bf16[256,1152]{1,0:T(8,128)(2,1)S(1)} %get-tuple-element.25), channel_id=1, source_target_pairs={{0,2},{2,4},{4,6},{6,8},{8,10},{10,13},{12,15},{14,17},{16,19},{18... | collective-permute-start | bytes 1769480 | tf_op jit(solution)/shard_map/ppermute | solution.py:264
  22.2 8.8 %collective-permute-done.1.a1 = bf16[256,1152]{1,0:T(8,128)(2,1)S(1)} collective-permute-done((bf16[256,1152]{1,0:T(8,128)(2,1)S(1)}, bf16[256,1152]{1,0:T(8,128)(2,1)S(1)}, u32[]{:S(2)}, u32[]{:S(2)}) %collective-permute-start.1) | collective-permute-done | bytes 589856 | tf_op jit(solution)/shard_map/ppermute | solution.py:264
  30.9 6.6 %collective-permute-start.2 = (bf16[256,1152]{1,0:T(8,128)(2,1)S(1)}, bf16[256,1152]{1,0:T(8,128)(2,1)S(1)}, u32[]{:S(2)}, u32[]{:S(2)}) collective-permute-start(bf16[256,1152]{1,0:T(8,128)(2,1)S(1)} %collective-permute-done.1.a1), channel_id=1, source_target_pairs={{0,2},{2,4},{4,6},{6,8},{8,10},{10,13},{13,15},{15,17},{17,19},{19... | collective-permute-start | bytes 1769480 | tf_op jit(solution)/shard_map/ppermute | solution.py:264
  37.6 0.0 collective-permute-done.7.b1
  37.6 11.5 %collective-permute-start.8 = (bf16[256,1152]{1,0:T(8,128)(2,1)S(1)}, bf16[256,1152]{1,0:T(8,128)(2,1)S(1)}, u32[]{:S(2)}, u32[]{:S(2)}) collective-permute-start(bf16[256,1152]{1,0:T(8,128)(2,1)S(1)} %collective-permute-done.7.b1), channel_id=1, source_target_pairs={{0,2},{2,4},{4,6},{6,8},{8,10},{10,13},{13,15},{15,17},{17,19},{19... | collective-permute-start | bytes 1769480 | tf_op jit(solution)/shard_map/ppermute | solution.py:264
  49.1 0.0 collective-permute-done.2.a2
  49.1 3.1 %collective-permute-start.3 = (bf16[256,1152]{1,0:T(8,128)(2,1)S(1)}, bf16[256,1152]{1,0:T(8,128)(2,1)S(1)}, u32[]{:S(2)}, u32[]{:S(2)}) collective-permute-start(bf16[256,1152]{1,0:T(8,128)(2,1)S(1)} %collective-permute-done.2.a2), channel_id=1, source_target_pairs={{0,2},{2,4},{4,6},{6,8},{8,10},{10,13},{13,15},{15,17},{17,19},{19... | collective-permute-start | bytes 1769480 | tf_op jit(solution)/shard_map/ppermute | solution.py:264
  52.2 12.9 %collective-permute-done.mine = bf16[512,1152]{1,0:T(8,128)(2,1)S(1)} collective-permute-done((bf16[512,1152]{1,0:T(8,128)(2,1)S(1)}, bf16[512,1152]{1,0:T(8,128)(2,1)S(1)}, u32[]{:S(2)}, u32[]{:S(2)}) %collective-permute-start) | collective-permute-done | bytes 1179680 | tf_op jit(solution)/shard_map/ppermute | solution.py:264
  65.0 0.1 fusion
  65.1 1.9 %collective-permute-start.5 = (bf16[256,1152]{1,0:T(8,128)(2,1)S(1)}, bf16[256,1152]{1,0:T(8,128)(2,1)S(1)}, u32[]{:S(2)}, u32[]{:S(2)}) collective-permute-start(bf16[256,1152]{1,0:T(8,128)(2,1)S(1)} %get-tuple-element.44), channel_id=1, source_target_pairs={{0,24},{24,0},{2,26},{26,2},{4,28},{28,4},{6,30},{30,6},{8,32},{32... | collective-permute-start | bytes 1769480 | tf_op jit(solution)/shard_map/ppermute | solution.py:264
  67.0 2.4 %collective-permute-start.6 = (bf16[256,1152]{1,0:T(8,128)(2,1)S(1)}, bf16[256,1152]{1,0:T(8,128)(2,1)S(1)}, u32[]{:S(2)}, u32[]{:S(2)}) collective-permute-start(bf16[256,1152]{1,0:T(8,128)(2,1)S(1)} %get-tuple-element.43), channel_id=1, source_target_pairs={{0,24},{24,0},{2,26},{26,2},{4,28},{28,4},{6,30},{30,6},{8,32},{32... | collective-permute-start | bytes 1769480 | tf_op jit(solution)/shard_map/ppermute | solution.py:264
  69.4 0.0 collective-permute-done.8.b2
  69.5 1.9 %collective-permute-start.9 = (bf16[256,1152]{1,0:T(8,128)(2,1)S(1)}, bf16[256,1152]{1,0:T(8,128)(2,1)S(1)}, u32[]{:S(2)}, u32[]{:S(2)}) collective-permute-start(bf16[256,1152]{1,0:T(8,128)(2,1)S(1)} %collective-permute-done.8.b2), channel_id=1, source_target_pairs={{0,2},{2,4},{4,6},{6,8},{8,10},{10,13},{13,15},{15,17},{17,19},{19... | collective-permute-start | bytes 1769480 | tf_op jit(solution)/shard_map/ppermute | solution.py:264
  72.7 0.0 collective-permute-done.3.a3
  72.7 0.1 pad_maximum_fusion
  72.8 1.9 %collective-permute-start.4 = (bf16[288,1152]{1,0:T(8,128)(2,1)S(1)}, bf16[288,1152]{1,0:T(8,128)(2,1)S(1)}, u32[]{:S(2)}, u32[]{:S(2)}) collective-permute-start(bf16[288,1152]{1,0:T(8,128)(2,1)S(1)} %pad_maximum_fusion), channel_id=1, source_target_pairs={{0,2},{2,4},{4,6},{6,8},{8,10},{10,13},{13,15},{15,17},{17,19},{19... | collective-permute-start | bytes 1990664 | tf_op jit(solution)/shard_map/ppermute | solution.py:264
  74.7 0.1 pad_maximum_fusion.1.scalars
  74.8 0.0 collective-permute-done.5.low
  74.8 0.0 collective-permute-done.6.middle
  74.8 7.4 %shard_map.68 = (f32[2,256,1152]{2,1,0:T(8,128)S(1)}, f32[2,256,128]{2,1,0:T(8,128)S(1)}, f32[2,256,128]{2,1,0:T(8,128)S(1)}) custom-call(f32[2]{0:T(128)S(1)} %pad_maximum_fusion.1.scalars, bf16[512,1152]{1,0:T(8,128)(2,1)S(1)} %collective-permute-done.mine, bf16[256,1152]{1,0:T(8,128)(2,1)S(1)} %collective-permute-done.5.low, ...), custom_call_target="tpu_custom_call" | custom-call | flops 1 | bytes 1 | tf_op jit(solution)/shard_map/pallas_call | solution.py:210
  82.2 0.0 collective-permute-done.9.b3
  82.2 1.7 %shard_map.69 = bf16[256,1280]{1,0:T(8,128)(2,1)S(1)} custom-call(f32[2]{0:T(128)S(1)} %pad_maximum_fusion.1.scalars, bf16[256,1152]{1,0:T(8,128)(2,1)S(1)} %collective-permute-done.5.low, bf16[256,1152]{1,0:T(8,128)(2,1)S(1)} %collective-permute-done.6.middle, bf16[256,1152]{1,0:T(8,128)(2,1)S(1)} %collective-permute-done.3.a3, ...), custom_call_target="tpu_custom_call" | custom-call | flops 1 | bytes 1 | tf_op jit(solution)/shard_map/pallas_call | solution.py:210
  83.9 3.1 %collective-permute-start.10 = (bf16[256,1280]{1,0:T(8,128)(2,1)S(1)}, bf16[256,1280]{1,0:T(8,128)(2,1)S(1)}, u32[]{:S(2)}, u32[]{:S(2)}) collective-permute-start(bf16[256,1280]{1,0:T(8,128)(2,1)S(1)} %shard_map.69), channel_id=1, source_target_pairs={{0,1},{2,3},{4,5},{6,7},{8,9},{10,11},{13,13},{15,15},{17,17},{19,... | collective-permute-start | bytes 1966088 | tf_op jit(solution)/shard_map/ppermute | solution.py:264
  87.0 1.7 %shard_map.70 = (f32[256,1152]{1,0:T(8,128)S(1)}, f32[256,128]{1,0:T(8,128)S(1)}, f32[256,128]{1,0:T(8,128)S(1)}) custom-call(f32[2]{0:T(128)S(1)} %pad_maximum_fusion.1.scalars, bf16[512,1152]{1,0:T(8,128)(2,1)S(1)} %collective-permute-done.mine, bf16[256,1152]{1,0:T(8,128)(2,1)S(1)} %collective-permute-done.3.a3, ...), custom_call_target="tpu_custom_call" | custom-call | flops 1 | bytes 1 | tf_op jit(solution)/shard_map/pallas_call | solution.py:210
  88.8 0.0 collective-permute-done.4.a4
  88.8 0.0 copy-start.1
  88.8 0.0 copy-start.3
  88.8 1.6 %shard_map.71 = bf16[256,1280]{1,0:T(8,128)(2,1)S(1)} custom-call(f32[2]{0:T(128)S(1)} %pad_maximum_fusion.1.scalars, bf16[512,1152]{1,0:T(8,128)(2,1)S(1)} %collective-permute-done.mine, bf16[288,1152]{1,0:T(8,128)(2,1)S(1)} %collective-permute-done.4.a4, f32[256,1152]{1,0:T(8,128)S(1)} %get-tuple-element.31.acc, f32[256,128]{1,0:T(8,128)S(1)} %get-tuple-element.32.above, ...), custom_call_target="tpu_custom_call" | custom-call | flops 1 | bytes 1 | tf_op jit(solution)/shard_map/pallas_call | solution.py:210
  90.4 13.8 %collective-permute-done.10.block = bf16[256,1280]{1,0:T(8,128)(2,1)S(1)} collective-permute-done((bf16[256,1280]{1,0:T(8,128)(2,1)S(1)}, bf16[256,1280]{1,0:T(8,128)(2,1)S(1)}, u32[]{:S(2)}, u32[]{:S(2)}) %collective-permute-start.10) | collective-permute-done | bytes 655392 | tf_op jit(solution)/shard_map/ppermute | solution.py:264
  104.1 1.9 %collective-permute-start.11 = (bf16[256,1280]{1,0:T(8,128)(2,1)S(1)}, bf16[256,1280]{1,0:T(8,128)(2,1)S(1)}, u32[]{:S(2)}, u32[]{:S(2)}) collective-permute-start(bf16[256,1280]{1,0:T(8,128)(2,1)S(1)} %shard_map.71), channel_id=1, source_target_pairs={{0,0},{2,2},{4,4},{6,6},{8,8},{10,10},{13,12},{15,14},{17,16},{19,... | collective-permute-start | bytes 1966088 | tf_op jit(solution)/shard_map/ppermute | solution.py:264
  106.0 0.0 copy-done.1
  106.1 0.0 copy-done.3
  106.1 2.1 %shard_map.72 = (f32[256,1152]{1,0:T(8,128)}, f32[256,1152]{1,0:T(8,128)}, f32[1,256]{1,0:T(1,128)S(1)}) custom-call(s32[2]{0:T(128)S(1)} %pad_add_fusion.flags, bf16[256,1152]{1,0:T(8,128)(2,1)S(1)} %copy-done.1, bf16[256,1152]{1,0:T(8,128)(2,1)S(1)} %copy-done.3, bf16[256,1280]{1,0:T(8,128)(2,1)S(1)} %collective-permute-done.10.block), custom_call_target="tpu_custom_call" | custom-call | flops 1 | bytes 1 | tf_op jit(solution)/shard_map/pallas_call | solution.py:210
  108.2 7.9 %collective-permute-done.11.block = bf16[256,1280]{1,0:T(8,128)(2,1)S(1)} collective-permute-done((bf16[256,1280]{1,0:T(8,128)(2,1)S(1)}, bf16[256,1280]{1,0:T(8,128)(2,1)S(1)}, u32[]{:S(2)}, u32[]{:S(2)}) %collective-permute-start.11) | collective-permute-done | bytes 655392 | tf_op jit(solution)/shard_map/ppermute | solution.py:264
  116.0 2.7 %shard_map.73 = (f32[256,1152]{1,0:T(8,128)}, f32[256,1152]{1,0:T(8,128)}, f32[1,256]{1,0:T(1,128)}) custom-call(s32[2]{0:T(128)S(1)} %pad_add_fusion.flags, bf16[256,1152]{1,0:T(8,128)(2,1)S(1)} %copy-done.1, bf16[256,1152]{1,0:T(8,128)(2,1)S(1)} %copy-done.3, ...), custom_call_target="tpu_custom_call", output_to_operand_aliasing={{0}: (5, {}), {1}: (6, {})} | custom-call | flops 1 | bytes 1 | tf_op jit(solution)/shard_map/pallas_call | solution.py:210
  (1 shorter events, 0.0 us)
Async XLA Ops:
  0.7 1.1 copy-start
  1.8 1.1 copy-start.2
  4.0 27.0 %collective-permute-start.1 = (bf16[256,1152]{1,0:T(8,128)(2,1)S(1)}, bf16[256,1152]{1,0:T(8,128)(2,1)S(1)}, u32[]{:S(2)}, u32[]{:S(2)}) collective-permute-start(bf16[256,1152]{1,0:T(8,128)(2,1)S(1)} %get-tuple-element.24), channel_id=1, source_target_pairs={{0,767},{2,24},{4,26},{6,28},{8,30},{10,32},{12,34},{14,37},{16,39... | collective-permute-start | bytes 1769480 | tf_op jit(solution)/shard_map/ppermute | solution.py:264
  18.3 46.7 %collective-permute-start = (bf16[512,1152]{1,0:T(8,128)(2,1)S(1)}, bf16[512,1152]{1,0:T(8,128)(2,1)S(1)}, u32[]{:S(2)}, u32[]{:S(2)}) collective-permute-start(bf16[512,1152]{1,0:T(8,128)(2,1)S(1)} %get-tuple-element.23), channel_id=1, source_target_pairs={{0,0},{1,24},{2,2},{3,26},{4,4},{5,28},{6,6},{7,30},{8,8},{9,32},{... | collective-permute-start | bytes 3538952 | tf_op jit(solution)/shard_map/ppermute | solution.py:264
  20.2 17.3 %collective-permute-start.7 = (bf16[256,1152]{1,0:T(8,128)(2,1)S(1)}, bf16[256,1152]{1,0:T(8,128)(2,1)S(1)}, u32[]{:S(2)}, u32[]{:S(2)}) collective-permute-start(bf16[256,1152]{1,0:T(8,128)(2,1)S(1)} %get-tuple-element.25), channel_id=1, source_target_pairs={{0,2},{2,4},{4,6},{6,8},{8,10},{10,13},{12,15},{14,17},{16,19},{18... | collective-permute-start | bytes 1769480 | tf_op jit(solution)/shard_map/ppermute | solution.py:264
  30.9 18.1 %collective-permute-start.2 = (bf16[256,1152]{1,0:T(8,128)(2,1)S(1)}, bf16[256,1152]{1,0:T(8,128)(2,1)S(1)}, u32[]{:S(2)}, u32[]{:S(2)}) collective-permute-start(bf16[256,1152]{1,0:T(8,128)(2,1)S(1)} %collective-permute-done.1.a1), channel_id=1, source_target_pairs={{0,2},{2,4},{4,6},{6,8},{8,10},{10,13},{13,15},{15,17},{17,19},{19... | collective-permute-start | bytes 1769480 | tf_op jit(solution)/shard_map/ppermute | solution.py:264
  37.6 31.9 %collective-permute-start.8 = (bf16[256,1152]{1,0:T(8,128)(2,1)S(1)}, bf16[256,1152]{1,0:T(8,128)(2,1)S(1)}, u32[]{:S(2)}, u32[]{:S(2)}) collective-permute-start(bf16[256,1152]{1,0:T(8,128)(2,1)S(1)} %collective-permute-done.7.b1), channel_id=1, source_target_pairs={{0,2},{2,4},{4,6},{6,8},{8,10},{10,13},{13,15},{15,17},{17,19},{19... | collective-permute-start | bytes 1769480 | tf_op jit(solution)/shard_map/ppermute | solution.py:264
  49.1 23.6 %collective-permute-start.3 = (bf16[256,1152]{1,0:T(8,128)(2,1)S(1)}, bf16[256,1152]{1,0:T(8,128)(2,1)S(1)}, u32[]{:S(2)}, u32[]{:S(2)}) collective-permute-start(bf16[256,1152]{1,0:T(8,128)(2,1)S(1)} %collective-permute-done.2.a2), channel_id=1, source_target_pairs={{0,2},{2,4},{4,6},{6,8},{8,10},{10,13},{13,15},{15,17},{17,19},{19... | collective-permute-start | bytes 1769480 | tf_op jit(solution)/shard_map/ppermute | solution.py:264
  65.1 9.7 %collective-permute-start.5 = (bf16[256,1152]{1,0:T(8,128)(2,1)S(1)}, bf16[256,1152]{1,0:T(8,128)(2,1)S(1)}, u32[]{:S(2)}, u32[]{:S(2)}) collective-permute-start(bf16[256,1152]{1,0:T(8,128)(2,1)S(1)} %get-tuple-element.44), channel_id=1, source_target_pairs={{0,24},{24,0},{2,26},{26,2},{4,28},{28,4},{6,30},{30,6},{8,32},{32... | collective-permute-start | bytes 1769480 | tf_op jit(solution)/shard_map/ppermute | solution.py:264
  67.0 7.7 %collective-permute-start.6 = (bf16[256,1152]{1,0:T(8,128)(2,1)S(1)}, bf16[256,1152]{1,0:T(8,128)(2,1)S(1)}, u32[]{:S(2)}, u32[]{:S(2)}) collective-permute-start(bf16[256,1152]{1,0:T(8,128)(2,1)S(1)} %get-tuple-element.43), channel_id=1, source_target_pairs={{0,24},{24,0},{2,26},{26,2},{4,28},{28,4},{6,30},{30,6},{8,32},{32... | collective-permute-start | bytes 1769480 | tf_op jit(solution)/shard_map/ppermute | solution.py:264
  69.5 12.7 %collective-permute-start.9 = (bf16[256,1152]{1,0:T(8,128)(2,1)S(1)}, bf16[256,1152]{1,0:T(8,128)(2,1)S(1)}, u32[]{:S(2)}, u32[]{:S(2)}) collective-permute-start(bf16[256,1152]{1,0:T(8,128)(2,1)S(1)} %collective-permute-done.8.b2), channel_id=1, source_target_pairs={{0,2},{2,4},{4,6},{6,8},{8,10},{10,13},{13,15},{15,17},{17,19},{19... | collective-permute-start | bytes 1769480 | tf_op jit(solution)/shard_map/ppermute | solution.py:264
  72.8 16.0 %collective-permute-start.4 = (bf16[288,1152]{1,0:T(8,128)(2,1)S(1)}, bf16[288,1152]{1,0:T(8,128)(2,1)S(1)}, u32[]{:S(2)}, u32[]{:S(2)}) collective-permute-start(bf16[288,1152]{1,0:T(8,128)(2,1)S(1)} %pad_maximum_fusion), channel_id=1, source_target_pairs={{0,2},{2,4},{4,6},{6,8},{8,10},{10,13},{13,15},{15,17},{17,19},{19... | collective-permute-start | bytes 1990664 | tf_op jit(solution)/shard_map/ppermute | solution.py:264
  83.9 20.2 %collective-permute-start.10 = (bf16[256,1280]{1,0:T(8,128)(2,1)S(1)}, bf16[256,1280]{1,0:T(8,128)(2,1)S(1)}, u32[]{:S(2)}, u32[]{:S(2)}) collective-permute-start(bf16[256,1280]{1,0:T(8,128)(2,1)S(1)} %shard_map.69), channel_id=1, source_target_pairs={{0,1},{2,3},{4,5},{6,7},{8,9},{10,11},{13,13},{15,15},{17,17},{19,... | collective-permute-start | bytes 1966088 | tf_op jit(solution)/shard_map/ppermute | solution.py:264
  88.8 17.3 %copy-start.1 = (bf16[256,1152]{1,0:T(8,128)(2,1)S(1)}, bf16[256,1152]{1,0:T(8,128)(2,1)}, u32[]{:S(2)}) copy-start(bf16[256,1152]{1,0:T(8,128)(2,1)} %images.5) | copy-start | bytes 1769476
  88.8 17.3 %copy-start.3 = (bf16[256,1152]{1,0:T(8,128)(2,1)S(1)}, bf16[256,1152]{1,0:T(8,128)(2,1)}, u32[]{:S(2)}) copy-start(bf16[256,1152]{1,0:T(8,128)(2,1)} %texts.5) | copy-start | bytes 1769476
  104.1 11.9 %collective-permute-start.11 = (bf16[256,1280]{1,0:T(8,128)(2,1)S(1)}, bf16[256,1280]{1,0:T(8,128)(2,1)S(1)}, u32[]{:S(2)}, u32[]{:S(2)}) collective-permute-start(bf16[256,1280]{1,0:T(8,128)(2,1)S(1)} %shard_map.71), channel_id=1, source_target_pairs={{0,0},{2,2},{4,4},{6,6},{8,8},{10,10},{13,12},{15,14},{17,16},{19,... | collective-permute-start | bytes 1966088 | tf_op jit(solution)/shard_map/ppermute | solution.py:264

commit v5 on v4

--- a/solution.py
+++ b/solution.py
@@ -154,7 +154,7 @@
     return inverse * (grad - unit * along)
 
 
-def write_grad(is_image, images, texts, block, grad_images, grad_texts, buf, sem):
+def write_grad(is_image, images, texts, block, grad_images, grad_texts, buf, sem, meanwhile):
     rows, width = images.shape
     count = rows // PIECES
 
@@ -173,6 +173,7 @@
             part = slice(at * count, (at + 1) * count)
             buf[part] = back_norm(raw[part], block[part, :width].astype(F32))
             copy.start()
+        meanwhile()
         for copy in copies(out):
             copy.wait()
 
@@ -181,8 +182,10 @@
 
 
 def finish_first_kernel(flags, images, texts, block, grad_images, grad_texts, loss, buf, sem):
-    loss[...] = as_row(loss_in(block, images.shape[1]))
-    write_grad(flags[1] == 1, images, texts, block, grad_images, grad_texts, buf, sem)
+    def write_loss():
+        loss[...] = as_row(loss_in(block, images.shape[1]))
+
+    write_grad(flags[1] == 1, images, texts, block, grad_images, grad_texts, buf, sem, write_loss)
 
 
 def finish_second_kernel(
@@ -199,10 +202,12 @@
     buf,
     sem,
 ):
-    loss[...] = jnp.where(
-        flags[1] == 1, loss_first[...], as_row(loss_in(block, images.shape[1]))
-    )
-    write_grad(flags[1] == 0, images, texts, block, grad_images, grad_texts, buf, sem)
+    def write_loss():
+        loss[...] = jnp.where(
+            flags[1] == 1, loss_first[...], as_row(loss_in(block, images.shape[1]))
+        )
+
+    write_grad(flags[1] == 0, images, texts, block, grad_images, grad_texts, buf, sem, write_loss)
 
 
 def call(kernel, outs, n_smem, args, in_hbm=0, outs_hbm=0, scratch=(), aliases=None, us=0.0):

time: 119 us -> 119 us (level)
  no operation moved by 1% of the time
where the time goes in v5:
time: 119 us
  starting transfers between devices  52.5 us (44%)
  waiting for transfers between devices  43.4 us (36%)
  Pallas kernels  18 us (15%)
  local copies, waits for them, and re-layouts  2.24 us (2%)
  between operations  2.19 us (2%)
    ppermute x12, starting transfers between devices, on_device(): move = lambda block, route: lax.ppermute(block, AXES, route)  52.5 us
    ppermute x12, waiting for transfers between devices, on_device(): move = lambda block, route: lax.ppermute(block, AXES, route)  43.4 us
    pallas_call x7, Pallas kernels, call(): pl.pallas_call(kernel, out_shape=outs, in_specs=smem(n_smem) + vmem(len(a...  18 us
  transfers between devices with their start and end apart: 12, of which 4 were waited for; matrix products, arithmetic and copies ran while one was open for 0% of the time, Pallas kernels for 12%

profile of v5, /device:TPU:3, one launch (start us, length us, event | category | flops | bytes accessed | tf_op | source)
XLA Modules:
  0.0 118.5 jit_solution(16397176703074242672)
XLA Ops:
  0.7 0.1 pad_add_fusion.flags
  0.7 0.0 copy-start
  0.7 1.1 copy-done
  1.8 0.0 copy-start.2
  1.8 1.1 copy-done.2
  2.9 1.1 shard_map.67
  4.0 14.3 %collective-permute-start.1 = (bf16[256,1152]{1,0:T(8,128)(2,1)S(1)}, bf16[256,1152]{1,0:T(8,128)(2,1)S(1)}, u32[]{:S(2)}, u32[]{:S(2)}) collective-permute-start(bf16[256,1152]{1,0:T(8,128)(2,1)S(1)} %get-tuple-element.24), channel_id=1, source_target_pairs={{0,767},{2,24},{4,26},{6,28},{8,30},{10,32},{12,34},{14,37},{16,39... | collective-permute-start | bytes 1769480 | tf_op jit(solution)/shard_map/ppermute | solution.py:269
  18.3 1.9 %collective-permute-start = (bf16[512,1152]{1,0:T(8,128)(2,1)S(1)}, bf16[512,1152]{1,0:T(8,128)(2,1)S(1)}, u32[]{:S(2)}, u32[]{:S(2)}) collective-permute-start(bf16[512,1152]{1,0:T(8,128)(2,1)S(1)} %get-tuple-element.23), channel_id=1, source_target_pairs={{0,0},{1,24},{2,2},{3,26},{4,4},{5,28},{6,6},{7,30},{8,8},{9,32},{... | collective-permute-start | bytes 3538952 | tf_op jit(solution)/shard_map/ppermute | solution.py:269
  20.2 1.9 %collective-permute-start.7 = (bf16[256,1152]{1,0:T(8,128)(2,1)S(1)}, bf16[256,1152]{1,0:T(8,128)(2,1)S(1)}, u32[]{:S(2)}, u32[]{:S(2)}) collective-permute-start(bf16[256,1152]{1,0:T(8,128)(2,1)S(1)} %get-tuple-element.25), channel_id=1, source_target_pairs={{0,2},{2,4},{4,6},{6,8},{8,10},{10,13},{12,15},{14,17},{16,19},{18... | collective-permute-start | bytes 1769480 | tf_op jit(solution)/shard_map/ppermute | solution.py:269
  22.2 8.8 %collective-permute-done.1.a1 = bf16[256,1152]{1,0:T(8,128)(2,1)S(1)} collective-permute-done((bf16[256,1152]{1,0:T(8,128)(2,1)S(1)}, bf16[256,1152]{1,0:T(8,128)(2,1)S(1)}, u32[]{:S(2)}, u32[]{:S(2)}) %collective-permute-start.1) | collective-permute-done | bytes 589856 | tf_op jit(solution)/shard_map/ppermute | solution.py:269
  30.9 6.6 %collective-permute-start.2 = (bf16[256,1152]{1,0:T(8,128)(2,1)S(1)}, bf16[256,1152]{1,0:T(8,128)(2,1)S(1)}, u32[]{:S(2)}, u32[]{:S(2)}) collective-permute-start(bf16[256,1152]{1,0:T(8,128)(2,1)S(1)} %collective-permute-done.1.a1), channel_id=1, source_target_pairs={{0,2},{2,4},{4,6},{6,8},{8,10},{10,13},{13,15},{15,17},{17,19},{19... | collective-permute-start | bytes 1769480 | tf_op jit(solution)/shard_map/ppermute | solution.py:269
  37.6 0.0 collective-permute-done.7.b1
  37.6 11.5 %collective-permute-start.8 = (bf16[256,1152]{1,0:T(8,128)(2,1)S(1)}, bf16[256,1152]{1,0:T(8,128)(2,1)S(1)}, u32[]{:S(2)}, u32[]{:S(2)}) collective-permute-start(bf16[256,1152]{1,0:T(8,128)(2,1)S(1)} %collective-permute-done.7.b1), channel_id=1, source_target_pairs={{0,2},{2,4},{4,6},{6,8},{8,10},{10,13},{13,15},{15,17},{17,19},{19... | collective-permute-start | bytes 1769480 | tf_op jit(solution)/shard_map/ppermute | solution.py:269
  49.1 0.0 collective-permute-done.2.a2
  49.1 3.1 %collective-permute-start.3 = (bf16[256,1152]{1,0:T(8,128)(2,1)S(1)}, bf16[256,1152]{1,0:T(8,128)(2,1)S(1)}, u32[]{:S(2)}, u32[]{:S(2)}) collective-permute-start(bf16[256,1152]{1,0:T(8,128)(2,1)S(1)} %collective-permute-done.2.a2), channel_id=1, source_target_pairs={{0,2},{2,4},{4,6},{6,8},{8,10},{10,13},{13,15},{15,17},{17,19},{19... | collective-permute-start | bytes 1769480 | tf_op jit(solution)/shard_map/ppermute | solution.py:269
  52.2 12.9 %collective-permute-done.mine = bf16[512,1152]{1,0:T(8,128)(2,1)S(1)} collective-permute-done((bf16[512,1152]{1,0:T(8,128)(2,1)S(1)}, bf16[512,1152]{1,0:T(8,128)(2,1)S(1)}, u32[]{:S(2)}, u32[]{:S(2)}) %collective-permute-start) | collective-permute-done | bytes 1179680 | tf_op jit(solution)/shard_map/ppermute | solution.py:269
  65.0 0.1 fusion
  65.1 1.9 %collective-permute-start.5 = (bf16[256,1152]{1,0:T(8,128)(2,1)S(1)}, bf16[256,1152]{1,0:T(8,128)(2,1)S(1)}, u32[]{:S(2)}, u32[]{:S(2)}) collective-permute-start(bf16[256,1152]{1,0:T(8,128)(2,1)S(1)} %get-tuple-element.44), channel_id=1, source_target_pairs={{0,24},{24,0},{2,26},{26,2},{4,28},{28,4},{6,30},{30,6},{8,32},{32... | collective-permute-start | bytes 1769480 | tf_op jit(solution)/shard_map/ppermute | solution.py:269
  67.0 2.4 %collective-permute-start.6 = (bf16[256,1152]{1,0:T(8,128)(2,1)S(1)}, bf16[256,1152]{1,0:T(8,128)(2,1)S(1)}, u32[]{:S(2)}, u32[]{:S(2)}) collective-permute-start(bf16[256,1152]{1,0:T(8,128)(2,1)S(1)} %get-tuple-element.43), channel_id=1, source_target_pairs={{0,24},{24,0},{2,26},{26,2},{4,28},{28,4},{6,30},{30,6},{8,32},{32... | collective-permute-start | bytes 1769480 | tf_op jit(solution)/shard_map/ppermute | solution.py:269
  69.4 0.0 collective-permute-done.8.b2
  69.5 1.9 %collective-permute-start.9 = (bf16[256,1152]{1,0:T(8,128)(2,1)S(1)}, bf16[256,1152]{1,0:T(8,128)(2,1)S(1)}, u32[]{:S(2)}, u32[]{:S(2)}) collective-permute-start(bf16[256,1152]{1,0:T(8,128)(2,1)S(1)} %collective-permute-done.8.b2), channel_id=1, source_target_pairs={{0,2},{2,4},{4,6},{6,8},{8,10},{10,13},{13,15},{15,17},{17,19},{19... | collective-permute-start | bytes 1769480 | tf_op jit(solution)/shard_map/ppermute | solution.py:269
  72.7 0.0 collective-permute-done.3.a3
  72.7 0.1 pad_maximum_fusion
  72.8 1.9 %collective-permute-start.4 = (bf16[288,1152]{1,0:T(8,128)(2,1)S(1)}, bf16[288,1152]{1,0:T(8,128)(2,1)S(1)}, u32[]{:S(2)}, u32[]{:S(2)}) collective-permute-start(bf16[288,1152]{1,0:T(8,128)(2,1)S(1)} %pad_maximum_fusion), channel_id=1, source_target_pairs={{0,2},{2,4},{4,6},{6,8},{8,10},{10,13},{13,15},{15,17},{17,19},{19... | collective-permute-start | bytes 1990664 | tf_op jit(solution)/shard_map/ppermute | solution.py:269
  74.7 0.1 pad_maximum_fusion.1.scalars
  74.8 0.0 collective-permute-done.5.low
  74.8 0.0 collective-permute-done.6.middle
  74.8 7.4 %shard_map.68 = (f32[2,256,1152]{2,1,0:T(8,128)S(1)}, f32[2,256,128]{2,1,0:T(8,128)S(1)}, f32[2,256,128]{2,1,0:T(8,128)S(1)}) custom-call(f32[2]{0:T(128)S(1)} %pad_maximum_fusion.1.scalars, bf16[512,1152]{1,0:T(8,128)(2,1)S(1)} %collective-permute-done.mine, bf16[256,1152]{1,0:T(8,128)(2,1)S(1)} %collective-permute-done.5.low, ...), custom_call_target="tpu_custom_call" | custom-call | flops 1 | bytes 1 | tf_op jit(solution)/shard_map/pallas_call | solution.py:215
  82.2 0.0 collective-permute-done.9.b3
  82.2 1.7 %shard_map.69 = bf16[256,1280]{1,0:T(8,128)(2,1)S(1)} custom-call(f32[2]{0:T(128)S(1)} %pad_maximum_fusion.1.scalars, bf16[256,1152]{1,0:T(8,128)(2,1)S(1)} %collective-permute-done.5.low, bf16[256,1152]{1,0:T(8,128)(2,1)S(1)} %collective-permute-done.6.middle, bf16[256,1152]{1,0:T(8,128)(2,1)S(1)} %collective-permute-done.3.a3, ...), custom_call_target="tpu_custom_call" | custom-call | flops 1 | bytes 1 | tf_op jit(solution)/shard_map/pallas_call | solution.py:215
  83.9 3.1 %collective-permute-start.10 = (bf16[256,1280]{1,0:T(8,128)(2,1)S(1)}, bf16[256,1280]{1,0:T(8,128)(2,1)S(1)}, u32[]{:S(2)}, u32[]{:S(2)}) collective-permute-start(bf16[256,1280]{1,0:T(8,128)(2,1)S(1)} %shard_map.69), channel_id=1, source_target_pairs={{0,1},{2,3},{4,5},{6,7},{8,9},{10,11},{13,13},{15,15},{17,17},{19,... | collective-permute-start | bytes 1966088 | tf_op jit(solution)/shard_map/ppermute | solution.py:269
  87.0 1.7 %shard_map.70 = (f32[256,1152]{1,0:T(8,128)S(1)}, f32[256,128]{1,0:T(8,128)S(1)}, f32[256,128]{1,0:T(8,128)S(1)}) custom-call(f32[2]{0:T(128)S(1)} %pad_maximum_fusion.1.scalars, bf16[512,1152]{1,0:T(8,128)(2,1)S(1)} %collective-permute-done.mine, bf16[256,1152]{1,0:T(8,128)(2,1)S(1)} %collective-permute-done.3.a3, ...), custom_call_target="tpu_custom_call" | custom-call | flops 1 | bytes 1 | tf_op jit(solution)/shard_map/pallas_call | solution.py:215
  88.8 0.0 collective-permute-done.4.a4
  88.8 0.0 copy-start.1
  88.8 0.0 copy-start.3
  88.8 1.6 %shard_map.71 = bf16[256,1280]{1,0:T(8,128)(2,1)S(1)} custom-call(f32[2]{0:T(128)S(1)} %pad_maximum_fusion.1.scalars, bf16[512,1152]{1,0:T(8,128)(2,1)S(1)} %collective-permute-done.mine, bf16[288,1152]{1,0:T(8,128)(2,1)S(1)} %collective-permute-done.4.a4, f32[256,1152]{1,0:T(8,128)S(1)} %get-tuple-element.31.acc, f32[256,128]{1,0:T(8,128)S(1)} %get-tuple-element.32.above, ...), custom_call_target="tpu_custom_call" | custom-call | flops 1 | bytes 1 | tf_op jit(solution)/shard_map/pallas_call | solution.py:215
  90.4 13.8 %collective-permute-done.10.block = bf16[256,1280]{1,0:T(8,128)(2,1)S(1)} collective-permute-done((bf16[256,1280]{1,0:T(8,128)(2,1)S(1)}, bf16[256,1280]{1,0:T(8,128)(2,1)S(1)}, u32[]{:S(2)}, u32[]{:S(2)}) %collective-permute-start.10) | collective-permute-done | bytes 655392 | tf_op jit(solution)/shard_map/ppermute | solution.py:269
  104.1 1.9 %collective-permute-start.11 = (bf16[256,1280]{1,0:T(8,128)(2,1)S(1)}, bf16[256,1280]{1,0:T(8,128)(2,1)S(1)}, u32[]{:S(2)}, u32[]{:S(2)}) collective-permute-start(bf16[256,1280]{1,0:T(8,128)(2,1)S(1)} %shard_map.71), channel_id=1, source_target_pairs={{0,0},{2,2},{4,4},{6,6},{8,8},{10,10},{13,12},{15,14},{17,16},{19,... | collective-permute-start | bytes 1966088 | tf_op jit(solution)/shard_map/ppermute | solution.py:269
  106.0 0.0 copy-done.1
  106.1 0.0 copy-done.3
  106.1 2.0 %shard_map.72 = (f32[256,1152]{1,0:T(8,128)}, f32[256,1152]{1,0:T(8,128)}, f32[1,256]{1,0:T(1,128)S(1)}) custom-call(s32[2]{0:T(128)S(1)} %pad_add_fusion.flags, bf16[256,1152]{1,0:T(8,128)(2,1)S(1)} %copy-done.1, bf16[256,1152]{1,0:T(8,128)(2,1)S(1)} %copy-done.3, bf16[256,1280]{1,0:T(8,128)(2,1)S(1)} %collective-permute-done.10.block), custom_call_target="tpu_custom_call" | custom-call | flops 1 | bytes 1 | tf_op jit(solution)/shard_map/pallas_call | solution.py:215
  108.0 8.0 %collective-permute-done.11.block = bf16[256,1280]{1,0:T(8,128)(2,1)S(1)} collective-permute-done((bf16[256,1280]{1,0:T(8,128)(2,1)S(1)}, bf16[256,1280]{1,0:T(8,128)(2,1)S(1)}, u32[]{:S(2)}, u32[]{:S(2)}) %collective-permute-start.11) | collective-permute-done | bytes 655392 | tf_op jit(solution)/shard_map/ppermute | solution.py:269
  116.0 2.5 %shard_map.73 = (f32[256,1152]{1,0:T(8,128)}, f32[256,1152]{1,0:T(8,128)}, f32[1,256]{1,0:T(1,128)}) custom-call(s32[2]{0:T(128)S(1)} %pad_add_fusion.flags, bf16[256,1152]{1,0:T(8,128)(2,1)S(1)} %copy-done.1, bf16[256,1152]{1,0:T(8,128)(2,1)S(1)} %copy-done.3, ...), custom_call_target="tpu_custom_call", output_to_operand_aliasing={{0}: (5, {}), {1}: (6, {})} | custom-call | flops 1 | bytes 1 | tf_op jit(solution)/shard_map/pallas_call | solution.py:215
  (1 shorter events, 0.0 us)
Async XLA Ops:
  0.7 1.1 copy-start
  1.8 1.1 copy-start.2
  4.0 27.0 %collective-permute-start.1 = (bf16[256,1152]{1,0:T(8,128)(2,1)S(1)}, bf16[256,1152]{1,0:T(8,128)(2,1)S(1)}, u32[]{:S(2)}, u32[]{:S(2)}) collective-permute-start(bf16[256,1152]{1,0:T(8,128)(2,1)S(1)} %get-tuple-element.24), channel_id=1, source_target_pairs={{0,767},{2,24},{4,26},{6,28},{8,30},{10,32},{12,34},{14,37},{16,39... | collective-permute-start | bytes 1769480 | tf_op jit(solution)/shard_map/ppermute | solution.py:269
  18.3 46.7 %collective-permute-start = (bf16[512,1152]{1,0:T(8,128)(2,1)S(1)}, bf16[512,1152]{1,0:T(8,128)(2,1)S(1)}, u32[]{:S(2)}, u32[]{:S(2)}) collective-permute-start(bf16[512,1152]{1,0:T(8,128)(2,1)S(1)} %get-tuple-element.23), channel_id=1, source_target_pairs={{0,0},{1,24},{2,2},{3,26},{4,4},{5,28},{6,6},{7,30},{8,8},{9,32},{... | collective-permute-start | bytes 3538952 | tf_op jit(solution)/shard_map/ppermute | solution.py:269
  20.2 17.3 %collective-permute-start.7 = (bf16[256,1152]{1,0:T(8,128)(2,1)S(1)}, bf16[256,1152]{1,0:T(8,128)(2,1)S(1)}, u32[]{:S(2)}, u32[]{:S(2)}) collective-permute-start(bf16[256,1152]{1,0:T(8,128)(2,1)S(1)} %get-tuple-element.25), channel_id=1, source_target_pairs={{0,2},{2,4},{4,6},{6,8},{8,10},{10,13},{12,15},{14,17},{16,19},{18... | collective-permute-start | bytes 1769480 | tf_op jit(solution)/shard_map/ppermute | solution.py:269
  30.9 18.1 %collective-permute-start.2 = (bf16[256,1152]{1,0:T(8,128)(2,1)S(1)}, bf16[256,1152]{1,0:T(8,128)(2,1)S(1)}, u32[]{:S(2)}, u32[]{:S(2)}) collective-permute-start(bf16[256,1152]{1,0:T(8,128)(2,1)S(1)} %collective-permute-done.1.a1), channel_id=1, source_target_pairs={{0,2},{2,4},{4,6},{6,8},{8,10},{10,13},{13,15},{15,17},{17,19},{19... | collective-permute-start | bytes 1769480 | tf_op jit(solution)/shard_map/ppermute | solution.py:269
  37.6 31.9 %collective-permute-start.8 = (bf16[256,1152]{1,0:T(8,128)(2,1)S(1)}, bf16[256,1152]{1,0:T(8,128)(2,1)S(1)}, u32[]{:S(2)}, u32[]{:S(2)}) collective-permute-start(bf16[256,1152]{1,0:T(8,128)(2,1)S(1)} %collective-permute-done.7.b1), channel_id=1, source_target_pairs={{0,2},{2,4},{4,6},{6,8},{8,10},{10,13},{13,15},{15,17},{17,19},{19... | collective-permute-start | bytes 1769480 | tf_op jit(solution)/shard_map/ppermute | solution.py:269
  49.1 23.6 %collective-permute-start.3 = (bf16[256,1152]{1,0:T(8,128)(2,1)S(1)}, bf16[256,1152]{1,0:T(8,128)(2,1)S(1)}, u32[]{:S(2)}, u32[]{:S(2)}) collective-permute-start(bf16[256,1152]{1,0:T(8,128)(2,1)S(1)} %collective-permute-done.2.a2), channel_id=1, source_target_pairs={{0,2},{2,4},{4,6},{6,8},{8,10},{10,13},{13,15},{15,17},{17,19},{19... | collective-permute-start | bytes 1769480 | tf_op jit(solution)/shard_map/ppermute | solution.py:269
  65.1 9.7 %collective-permute-start.5 = (bf16[256,1152]{1,0:T(8,128)(2,1)S(1)}, bf16[256,1152]{1,0:T(8,128)(2,1)S(1)}, u32[]{:S(2)}, u32[]{:S(2)}) collective-permute-start(bf16[256,1152]{1,0:T(8,128)(2,1)S(1)} %get-tuple-element.44), channel_id=1, source_target_pairs={{0,24},{24,0},{2,26},{26,2},{4,28},{28,4},{6,30},{30,6},{8,32},{32... | collective-permute-start | bytes 1769480 | tf_op jit(solution)/shard_map/ppermute | solution.py:269
  67.0 7.7 %collective-permute-start.6 = (bf16[256,1152]{1,0:T(8,128)(2,1)S(1)}, bf16[256,1152]{1,0:T(8,128)(2,1)S(1)}, u32[]{:S(2)}, u32[]{:S(2)}) collective-permute-start(bf16[256,1152]{1,0:T(8,128)(2,1)S(1)} %get-tuple-element.43), channel_id=1, source_target_pairs={{0,24},{24,0},{2,26},{26,2},{4,28},{28,4},{6,30},{30,6},{8,32},{32... | collective-permute-start | bytes 1769480 | tf_op jit(solution)/shard_map/ppermute | solution.py:269
  69.5 12.7 %collective-permute-start.9 = (bf16[256,1152]{1,0:T(8,128)(2,1)S(1)}, bf16[256,1152]{1,0:T(8,128)(2,1)S(1)}, u32[]{:S(2)}, u32[]{:S(2)}) collective-permute-start(bf16[256,1152]{1,0:T(8,128)(2,1)S(1)} %collective-permute-done.8.b2), channel_id=1, source_target_pairs={{0,2},{2,4},{4,6},{6,8},{8,10},{10,13},{13,15},{15,17},{17,19},{19... | collective-permute-start | bytes 1769480 | tf_op jit(solution)/shard_map/ppermute | solution.py:269
  72.8 16.0 %collective-permute-start.4 = (bf16[288,1152]{1,0:T(8,128)(2,1)S(1)}, bf16[288,1152]{1,0:T(8,128)(2,1)S(1)}, u32[]{:S(2)}, u32[]{:S(2)}) collective-permute-start(bf16[288,1152]{1,0:T(8,128)(2,1)S(1)} %pad_maximum_fusion), channel_id=1, source_target_pairs={{0,2},{2,4},{4,6},{6,8},{8,10},{10,13},{13,15},{15,17},{17,19},{19... | collective-permute-start | bytes 1990664 | tf_op jit(solution)/shard_map/ppermute | solution.py:269
  83.9 20.2 %collective-permute-start.10 = (bf16[256,1280]{1,0:T(8,128)(2,1)S(1)}, bf16[256,1280]{1,0:T(8,128)(2,1)S(1)}, u32[]{:S(2)}, u32[]{:S(2)}) collective-permute-start(bf16[256,1280]{1,0:T(8,128)(2,1)S(1)} %shard_map.69), channel_id=1, source_target_pairs={{0,1},{2,3},{4,5},{6,7},{8,9},{10,11},{13,13},{15,15},{17,17},{19,... | collective-permute-start | bytes 1966088 | tf_op jit(solution)/shard_map/ppermute | solution.py:269
  88.8 17.3 %copy-start.1 = (bf16[256,1152]{1,0:T(8,128)(2,1)S(1)}, bf16[256,1152]{1,0:T(8,128)(2,1)}, u32[]{:S(2)}) copy-start(bf16[256,1152]{1,0:T(8,128)(2,1)} %images.5) | copy-start | bytes 1769476
  88.8 17.3 %copy-start.3 = (bf16[256,1152]{1,0:T(8,128)(2,1)S(1)}, bf16[256,1152]{1,0:T(8,128)(2,1)}, u32[]{:S(2)}) copy-start(bf16[256,1152]{1,0:T(8,128)(2,1)} %texts.5) | copy-start | bytes 1769476
  104.1 11.9 %collective-permute-start.11 = (bf16[256,1280]{1,0:T(8,128)(2,1)S(1)}, bf16[256,1280]{1,0:T(8,128)(2,1)S(1)}, u32[]{:S(2)}, u32[]{:S(2)}) collective-permute-start(bf16[256,1280]{1,0:T(8,128)(2,1)S(1)} %shard_map.71), channel_id=1, source_target_pairs={{0,0},{2,2},{4,4},{6,6},{8,8},{10,10},{13,12},{15,14},{17,16},{19,... | collective-permute-start | bytes 1966088 | tf_op jit(solution)/shard_map/ppermute | solution.py:269
